TPU v7x, 256 devices: a whole 4x4x8 slice. The times are simulated.
256 devices in a mesh: row: 16 (over x, y), col: 16 (over z, core).
Axes of the slice: x: 4, y: 4, z: 8, core: 2. Of those that a mesh axis runs over, the one named last changes fastest.
Arguments:
- kernel: float32 [3, 16, 3, 16, 256, 256], P(None, 'row', None, 'col'), as said below
- pattern: int32 [3, 16, 3, 16], P(None, 'row', None, 'col'), may hold values 0 or 1
- factor_cot: float32 [3, 16, 3, 16, 256, 256], P(None, 'row', None, 'col'), may hold values from -6 to 6
Outputs:
- factor: float32 [3, 16, 3, 16, 256, 256], P(None, 'row', None, 'col')
- grad: float32 [3, 16, 3, 16, 256, 256], P(None, 'row', None, 'col')
Inputs may be any that keep to these rules, and one draw needn't show every extreme that they name: `kernel`: entries of blocks off the diagonal lie within -3 / sqrt(256) to 3 / sqrt(256). Diagonal blocks are 4 times the identity plus a symmetric part whose entries lie within -6 / sqrt(256) to 6 / sqrt(256).
All inputs are finite; a program needn't handle non-finite values. No bound on the sum of `pattern` on one device may be relied on, other than what follows from the above.
Results may differ from a plain program's by a relative error of at most 0.0001.
Values sent between devices are 32-bit elements; how exact they have to be, the bound alone decides.
No kernel may reach another device: no remote copies, remote signals or barrier semaphores. Data moves between devices by JAX's collectives and lax.ppermute only.
A program may use at most 128 MiB of HBM per device.

v0:
```python
import jax
import jax.numpy as jnp
from jax import lax
from jax.sharding import PartitionSpec as P

W = 32
STEPS = 2


highest = lax.Precision.HIGHEST


def spread(array, axis, root):
    mine = lax.axis_index(axis) == root
    return lax.psum(jnp.where(mine, array, jnp.zeros_like(array)), axis)


def apply_update(matrix, row_panel, col_panel, row_ids, col_ids, current, first_col, last_col):
    upd_mask = ((row_ids[:, None] >= col_ids[None, :]) & (col_ids[None, :] > current)).astype(
        jnp.float32
    )
    product = jnp.einsum("aij,bkj->abik", row_panel, col_panel, precision=highest)
    return matrix.at[:, first_col:last_col].add(-(upd_mask[:, :, None, None] * product))


def on_device(kernel, pattern, factor_cot):
    grid_rows = lax.axis_size("row")
    grid_cols = lax.axis_size("col")
    row_index = lax.axis_index("row")
    col_index = lax.axis_index("col")
    local_rows = kernel.shape[0]
    local_cols = kernel.shape[2]
    block_size = kernel.shape[-1]
    col_ratio = grid_cols // grid_rows
    pick_slot = col_index // grid_rows
    holder = col_index % grid_rows
    row_ids = jnp.arange(local_rows, dtype=jnp.int32) * grid_rows + row_index
    col_ids = jnp.arange(local_cols, dtype=jnp.int32) * grid_cols + col_index
    distance = row_ids[:, None] - col_ids[None, :]
    kept = (pattern.reshape(local_rows, local_cols) == 1) & (distance > 0) & (distance <= W)
    keep_mask = ((distance == 0) | kept).astype(jnp.float32)[:, :, None, None]
    matrix = kernel.reshape(local_rows, local_cols, block_size, block_size) * keep_mask
    identity = jnp.eye(block_size, dtype=jnp.float32)
    stored = []
    for current in range(STEPS):
        root_row = current % grid_rows
        root_col = current % grid_cols
        diag_lr = current // grid_rows
        diag_lc = current // grid_cols
        is_owner = (row_index == root_row) & (col_index == root_col)
        diag_block = jnp.where(is_owner, matrix[diag_lr, diag_lc], identity)
        factor = jnp.linalg.cholesky(diag_block)
        inverse = jax.scipy.linalg.solve_triangular(factor, identity, lower=True)
        raw_panel = matrix[:, diag_lc]
        below_mask = (row_ids > current).astype(jnp.float32)[:, None, None]
        factor_b, inverse_b = (spread(factor, "row", root_row), spread(inverse, "row", root_row))
        solved = jnp.einsum("aij,kj->aik", raw_panel, inverse_b, precision=highest) * below_mask
        row_panel = spread(solved, "col", root_col)
        subset = lax.dynamic_index_in_dim(
            row_panel.reshape(local_cols, col_ratio, block_size, block_size),
            pick_slot,
            1,
            keepdims=False,
        )
        col_panel = spread(subset, "row", holder)
        stored.append((row_panel, col_panel, inverse_b, factor_b, diag_block))
        matrix = apply_update(
            matrix, row_panel, col_panel, row_ids, col_ids, current, 0, local_cols
        )
    factor_out = matrix
    for current in range(STEPS):
        row_panel, col_panel, inverse_b, factor_b, diag_block = stored[current]
        diag_lc = current // grid_cols
        column = row_panel + (row_ids == current).astype(jnp.float32)[:, None, None] * factor_b
        factor_out = factor_out.at[:, diag_lc].set(
            jnp.where(col_index == current % grid_cols, column, factor_out[:, diag_lc])
        )
    cot_local = factor_cot.reshape(local_rows, local_cols, block_size, block_size)
    gradient = cot_local * (col_ids >= STEPS).astype(jnp.float32)[None, :, None, None]
    for current in reversed(range(STEPS)):
        row_panel, col_panel, inverse_b, factor_b, diag_block = stored[current]
        root_row = current % grid_rows
        root_col = current % grid_cols
        diag_lr = current // grid_rows
        diag_lc = current // grid_cols
        is_owner = (row_index == root_row) & (col_index == root_col)
        below_mask = (row_ids > current).astype(jnp.float32)[:, None, None]
        upd_mask = ((row_ids[:, None] >= col_ids[None, :]) & (col_ids[None, :] > current)).astype(
            jnp.float32
        )
        masked = gradient * upd_mask[:, :, None, None]
        row_part = -jnp.einsum("abij,bjk->aik", masked, col_panel, precision=highest)
        col_part = -jnp.einsum("abji,ajk->bik", masked, row_panel, precision=highest)
        col_total = lax.psum(col_part, "row")
        placed = jnp.zeros((local_cols, col_ratio, block_size, block_size), jnp.float32)
        placed = lax.dynamic_update_index_in_dim(placed, col_total[:, None], pick_slot, 1)
        placed = placed.reshape(local_rows, block_size, block_size) * (row_index == holder).astype(
            jnp.float32
        )
        row_source = row_part + placed
        bar_panel = lax.psum(row_source, "col")
        bar_panel = (bar_panel + cot_local[:, diag_lc]) * below_mask
        panel_grad = jnp.einsum("aij,jk->aik", bar_panel, inverse_b, precision=highest)
        partial_value = -jnp.einsum("aji,ajk->ik", panel_grad, row_panel, precision=highest)
        bar_factor = lax.psum(partial_value, "row") + cot_local[diag_lr, diag_lc]
        pull_back = jax.vjp(jnp.linalg.cholesky, diag_block)[1]
        bar_block = pull_back(bar_factor)[0]
        gradient = gradient.at[:, diag_lc].add(jnp.where(col_index == root_col, panel_grad, 0.0))
        gradient = gradient.at[diag_lr, diag_lc].add(jnp.where(is_owner, bar_block, 0.0))
    grad_out = gradient * keep_mask
    return (factor_out.reshape(kernel.shape), grad_out.reshape(kernel.shape))


def solution(mesh):
    return jax.shard_map(
        on_device,
        mesh=mesh,
        in_specs=(
            P(None, "row", None, "col", None, None),
            P(None, "row", None, "col"),
            P(None, "row", None, "col", None, None),
        ),
        out_specs=(
            P(None, "row", None, "col", None, None),
            P(None, "row", None, "col", None, None),
        ),
        check_vma=False,
    )
```

profile of v0, /device:TPU:1, one launch (start us, length us, event | category | flops | bytes accessed | tf_op | source)
XLA Modules:
  0.0 1361.3 jit_solution(2110793934449503150)
XLA Ops:
  8.7 2.0 bitcast_multiply_fusion.2
  11.3 11.7 custom-call.35
  23.7 10.6 custom-call.36
  35.6 1.8 convolution_subtract_fusion.8
  37.4 1.6 copy.14
  38.9 12.5 custom-call.37
  54.1 1.7 fusion.96
  56.5 4.3 while.18
  61.6 20.5 %custom-call.38 = f32[2,128,128]{1,2,0:T(8,128)S(1)} custom-call(f32[2,128,128]{2,1,0:T(8,128)} %copy-done.27), custom_call_target="InvertDiagBlocksLowerTriangular" | custom-call | tf_op jit(solution)/shard_map/jit(_solve_triangular)/triangular_solve | solution.py:53
  83.8 96.9 %all-reduce.15.cloned.1.call-done = f32[256,256]{1,0:T(8,128)} async-done(((f32[256,256]{1,0:T(8,128)}), f32[256,256]{1,0:T(8,128)}) %all-reduce.15.cloned.1.call-update) | async-done | bytes 262160 | tf_op jit(solution)/shard_map/psum | solution.py:15
  180.7 2.6 fusion.41
  183.4 111.5 %all-reduce.17.cloned.1.call-done = f32[3,256,256]{2,1,0:T(8,128)} async-done(((f32[3,256,256]{2,1,0:T(8,128)}), f32[3,256,256]{2,1,0:T(8,128)}) %all-reduce.17.cloned.1.call-update) | async-done | bytes 786448 | tf_op jit(solution)/shard_map/psum | solution.py:15
  296.1 97.9 %all-reduce.19.cloned.1.call-done = f32[3,256,256]{2,1,0:T(8,128)} async-done(((f32[3,256,256]{2,1,0:T(8,128)}), f32[3,256,256]{2,1,0:T(8,128)}) %all-reduce.19.cloned.1.call-update) | async-done | bytes 786448 | tf_op jit(solution)/shard_map/psum | solution.py:15
  394.0 3.4 fusion.1
  397.4 2.0 copy_add_fusion.1
  400.2 1.9 copy.20
  404.5 12.5 custom-call.39
  417.1 10.4 custom-call.40
  429.4 1.8 convolution_subtract_fusion.7
  432.8 11.9 custom-call.41
  444.7 1.5 bitcast_dynamic-update-slice_fusion.7
  449.3 1.8 fusion.97
  451.1 7.0 while.19
  452.4 2.2 bitcast_dynamic-update-slice_fusion.13
  455.9 2.1 bitcast_dynamic-update-slice_fusion.13
  458.7 20.5 %custom-call.42 = f32[2,128,128]{1,2,0:T(8,128)S(1)} custom-call(f32[2,128,128]{2,1,0:T(8,128)} %copy-done.28), custom_call_target="InvertDiagBlocksLowerTriangular" | custom-call | tf_op jit(solution)/shard_map/jit(_solve_triangular)/triangular_solve | solution.py:53
  481.8 93.8 %all-reduce.21.cloned.1.call-done = f32[256,256]{1,0:T(8,128)} async-done(((f32[256,256]{1,0:T(8,128)}), f32[256,256]{1,0:T(8,128)}) %all-reduce.21.cloned.1.call-update) | async-done | bytes 262160 | tf_op jit(solution)/shard_map/psum | solution.py:15
  575.6 2.7 fusion.40
  578.4 2.0 broadcast_multiply_fusion
  580.4 109.2 %all-reduce.23.cloned.1.call-done = f32[3,256,256]{2,1,0:T(8,128)} async-done(((f32[3,256,256]{2,1,0:T(8,128)}), f32[3,256,256]{2,1,0:T(8,128)}) %all-reduce.23.cloned.1.call-update) | async-done | bytes 786448 | tf_op jit(solution)/shard_map/psum | solution.py:15
  690.6 6.0 fusion.28
  698.6 11.7 custom-call.47
  710.8 9.8 custom-call.48
  720.7 74.0 %all-reduce.35.cloned.1.call-done = (f32[3,256,256]{2,1,0:T(8,128)}, f32[3,256,256]{2,1,0:T(8,128)}) async-done(((f32[3,256,256]{2,1,0:T(8,128)}, f32[3,256,256]{2,1,0:T(8,128)}), (f32[3,256,256]{2,1,0:T(8,128)}, f32[3,256,256]{2,1,0:T(8,128)})) %all-reduce.35.cloned.1.call-update) | async-done | bytes 1572880 | tf_op jit(solution)/shard_map/psum | solution.py:15
  794.6 4.3 fusion.34
  799.0 1.7 fusion.118
  800.7 3.3 copy.69
  804.1 1.6 copy.42
  805.6 1.6 pad.37
  807.2 1.8 convolution_subtract_fusion.6
  809.0 101.5 %all-reduce.25.cloned.1.call-done = f32[3,256,256]{2,1,0:T(8,128)} async-done(((f32[3,256,256]{2,1,0:T(8,128)}), f32[3,256,256]{2,1,0:T(8,128)}) %all-reduce.25.cloned.1.call-update) | async-done | bytes 786448 | tf_op jit(solution)/shard_map/psum | solution.py:101
  910.6 3.1 fusion.52
  913.7 2.1 fusion.51
  917.5 91.9 %all-reduce.27.cloned.1.call-done = f32[256,256]{1,0:T(8,128)} async-done(((f32[256,256]{1,0:T(8,128)}), f32[256,256]{1,0:T(8,128)}) %all-reduce.27.cloned.1.call-update) | async-done | bytes 262160 | tf_op jit(solution)/shard_map/psum | solution.py:105
  1009.4 1.6 fusion.49
  1015.3 1.8 copy.38
  1020.2 4.8 fusion.22
  1025.7 12.5 custom-call.49
  1042.5 78.2 %all-reduce.29.cloned.1.call-done = f32[3,256,256]{2,1,0:T(8,128)} async-done(((f32[3,256,256]{2,1,0:T(8,128)}), f32[3,256,256]{2,1,0:T(8,128)}) %all-reduce.29.cloned.1.call-update) | async-done | bytes 786448 | tf_op jit(solution)/shard_map/psum | solution.py:94
  1120.7 4.3 fusion.37
  1125.3 5.6 while.20
  1126.6 1.5 bitcast_dynamic-update-slice_fusion.14
  1129.4 1.5 bitcast_dynamic-update-slice_fusion.14
  1131.6 20.5 %custom-call.50 = f32[2,128,128]{1,2,0:T(8,128)S(1)} custom-call(f32[2,128,128]{2,1,0:T(8,128)} %copy-done.26), custom_call_target="InvertDiagBlocksLowerTriangular" | custom-call | tf_op jit(solution)/shard_map/transpose(jvp(jit(cholesky)))/triangular_solve | solution.py:106
  1152.1 84.7 %all-reduce.31.cloned.1.call-done = f32[3,256,256]{2,1,0:T(8,128)} async-done(((f32[3,256,256]{2,1,0:T(8,128)}), f32[3,256,256]{2,1,0:T(8,128)}) %all-reduce.31.cloned.1.call-update) | async-done | bytes 786448 | tf_op jit(solution)/shard_map/psum | solution.py:101
  1236.8 3.5 constant_dynamic-update-slice_fusion
  1240.3 2.2 fusion.50
  1243.0 3.8 fusion
  1247.2 1.4 copy-done.3
  1248.6 1.4 copy.106
  1250.0 88.3 %all-reduce.33.cloned.1.call-done = (f32[256,256]{1,0:T(8,128)}, f32[256,256]{1,0:T(8,128)}, f32[256,256]{1,0:T(8,128)}) async-done(((f32[256,256]{1,0:T(8,128)}, f32[256,256]{1,0:T(8,128)}, f32[256,256]{1,0:T(8,128)}), (f32[256,256]{1,0:T(8,128)}, f32[256,256]{1,0:T(8,128)}, f32[256,256]{1,0:T(8,128)})) %all-reduce.33.cloned.1.call-update) | async-done | bytes 786448 | tf_op jit(solution)/shard_map/psum | solution.py:15
  1338.3 1.6 fusion.47
  1344.2 1.8 copy.44
  1349.3 1.6 copy.47
  (192 shorter events, 59.6 us)
Async XLA Ops:
  7.2 173.5 %all-reduce.15.cloned.1.call-start = ((), (), s32[]{:S(2)}) async-start(), calls=%async_computation | async-start | bytes 524288 | tf_op jit(solution)/shard_map/psum | solution.py:15
  11.0 45.5 %copy-start.7 = (f32[256,256]{0,1:T(8,128)}, f32[256,256]{0,1:T(8,128)S(1)}, u32[]{:S(2)}) copy-start(f32[256,256]{0,1:T(8,128)S(1)} %broadcast_select_fusion.2) | copy-start | bytes 786436
  11.2 71.5 %copy-start.9 = (f32[256,256]{1,0:T(8,128)}, f32[256,256]{1,0:T(8,128)S(1)}, u32[]{:S(2)}) copy-start(f32[256,256]{1,0:T(8,128)S(1)} %copy.11) | copy-start | bytes 786436
  11.2 12.5 copy-start.20
  51.5 2.6 copy-start.18
  60.9 0.7 copy-start.27
  61.6 234.4 %copy-start.33 = (s32[2,2]{1,0:T(2,128)}, s32[2,2]{1,0:T(2,128)S(1)}, u32[]{:S(2)}) copy-start(s32[2,2]{1,0:T(2,128)S(1)} %get-tuple-element.435) | copy-start | bytes 52
  83.7 211.3 %all-reduce.17.cloned.1.call-start = ((), (), s32[]{:S(2)}) async-start(), calls=%async_computation.1 | async-start | bytes 1572864 | tf_op jit(solution)/shard_map/psum | solution.py:15
  83.8 212.2 %copy-start.30 = (f32[3]{0:T(128)}, f32[3]{0:T(128)S(1)}, u32[]{:S(2)}) copy-start(f32[3]{0:T(128)S(1)} %compare_convert_fusion.4) | copy-start | bytes 40
  183.4 210.6 %all-reduce.19.cloned.1.call-start = ((), (), s32[]{:S(2)}) async-start(), calls=%async_computation.2 | async-start | bytes 1572864 | tf_op jit(solution)/shard_map/psum | solution.py:15
  295.0 99.0 %copy-start = (f32[3,256,256]{2,1,0:T(8,128)S(1)}, f32[3,256,256]{2,1,0:T(8,128)}, u32[]{:S(2)}) copy-start(f32[3,256,256]{2,1,0:T(8,128)} %all-reduce.17.cloned.1.call-done) | copy-start | bytes 2359300
  296.0 279.6 %all-reduce.21.cloned.1.call-start = ((), (), s32[]{:S(2)}) async-start(), calls=%async_computation.3 | async-start | bytes 524288 | tf_op jit(solution)/shard_map/psum | solution.py:15
  399.4 176.2 %copy-start.5 = (f32[3,3,256,256]{3,2,1,0:T(8,128)}, f32[3,3,256,256]{3,2,1,0:T(8,128)S(1)}, u32[]{:S(2)}) copy-start(f32[3,3,256,256]{3,2,1,0:T(8,128)S(1)} %copy_add_fusion.1) | copy-start | bytes 7077892
  403.1 0.7 copy-start.21
  458.1 0.7 copy-start.28
  479.2 532.4 %copy-start.13 = (f32[2,128,128]{1,2,0:T(8,128)}, f32[2,128,128]{1,2,0:T(8,128)S(1)}, u32[]{:S(2)}) copy-start(f32[2,128,128]{1,2,0:T(8,128)S(1)} %custom-call.42) | copy-start | bytes 393220
  481.7 207.9 %all-reduce.23.cloned.1.call-start = ((), (), s32[]{:S(2)}) async-start(), calls=%async_computation.4 | async-start | bytes 1572864 | tf_op jit(solution)/shard_map/psum | solution.py:15
  481.8 96.6 %copy-start.29 = (f32[3]{0:T(128)}, f32[3]{0:T(128)S(1)}, u32[]{:S(2)}) copy-start(f32[3]{0:T(128)S(1)} %compare_convert_fusion.3) | copy-start | bytes 40
  578.3 216.4 %all-reduce.35.cloned.1.call-start = ((), (), s32[]{:S(2)}) async-start(), calls=%async_computation.10 | async-start | bytes 3145728 | tf_op jit(solution)/shard_map/psum | solution.py:15
  690.6 6.3 copy-start.8
  696.6 214.0 %all-reduce.25.cloned.1.call-start = ((), (), s32[]{:S(2)}) async-start(), calls=%async_computation.5 | async-start | bytes 1572864 | tf_op jit(solution)/shard_map/psum | solution.py:101
  697.8 0.7 copy-start.19
  710.3 88.7 %copy-start.24 = (f32[128,128]{1,0:T(8,128)}, f32[128,128]{1,0:T(8,128)S(1)}, u32[]{:S(2)}) copy-start(f32[128,128]{1,0:T(8,128)S(1)} %custom-call.47) | copy-start | bytes 196612
  798.9 210.5 %all-reduce.27.cloned.1.call-start = ((), (), s32[]{:S(2)}) async-start(), calls=%async_computation.6 | async-start | bytes 524288 | tf_op jit(solution)/shard_map/psum | solution.py:105
  800.7 109.8 %copy-start.16 = (f32[256,256]{1,0:T(8,128)S(1)}, f32[256,256]{1,0:T(8,128)}, u32[]{:S(2)}) copy-start(f32[256,256]{1,0:T(8,128)} %all-reduce.21.cloned.1.call-done) | copy-start | bytes 786436
  910.5 3.2 copy-start.1
  915.8 95.5 %copy-start.10 = (f32[256,256]{1,0:T(8,128)S(1)}, f32[256,256]{1,0:T(8,128)}, u32[]{:S(2)}) copy-start(f32[256,256]{1,0:T(8,128)} %get-tuple-element.411) | copy-start | bytes 786436
  915.8 204.9 %all-reduce.29.cloned.1.call-start = ((), (), s32[]{:S(2)}) async-start(), calls=%async_computation.7 | async-start | bytes 1572864 | tf_op jit(solution)/shard_map/psum | solution.py:94
  1014.6 0.8 copy-start.15
  1020.1 4.9 copy-start.25
  1020.2 19.3 %copy-start.31 = (f32[128]{0:T(128)S(1)}, f32[128]{0:T(128)}, u32[]{:S(2)}) copy-start(f32[128]{0:T(128)} %get-tuple-element.218) | copy-start | bytes 1540
  1025.0 211.8 %all-reduce.31.cloned.1.call-start = ((), (), s32[]{:S(2)}) async-start(), calls=%async_computation.8 | async-start | bytes 1572864 | tf_op jit(solution)/shard_map/psum | solution.py:101
  1125.0 213.3 %all-reduce.33.cloned.1.call-start = ((), (), s32[]{:S(2)}) async-start(), calls=%async_computation.9 | async-start | bytes 1572864 | tf_op jit(solution)/shard_map/psum | solution.py:15
  1130.9 0.6 copy-start.26
  1152.0 188.4 %copy-start.22 = (f32[2,128,128]{1,2,0:T(8,128)}, f32[2,128,128]{1,2,0:T(8,128)S(1)}, u32[]{:S(2)}) copy-start(f32[2,128,128]{1,2,0:T(8,128)S(1)} %custom-call.50) | copy-start | bytes 393220
  1242.5 4.3 copy-start.6
  1247.2 1.4 copy-start.3
  1343.4 0.7 copy-start.14
  1349.0 1.9 copy-start.17
  1349.3 2.5 copy-start.4
  1349.3 3.2 copy-start.11
  1350.9 2.0 copy-start.2
  1350.9 2.0 copy-start.23
  1350.9 2.0 copy-start.32
  1353.1 1.4 copy-start.12
Sparse Core Ops, SparseCore 0:
  83.8 96.8 all-reduce.14
  183.7 111.2 all-reduce.16
  298.8 95.1 all-reduce.18
  481.8 93.7 all-reduce.20
  578.4 111.2 all-reduce.22
  696.7 97.8 all-reduce.34
  799.1 111.4 all-reduce.24
  916.0 93.4 all-reduce.26
  1025.1 95.5 all-reduce.28
  1125.1 111.5 all-reduce.30
  1242.6 95.5 all-reduce.32
where the time goes:
time: 1380 us; the launch traced here: 1360 us
  waiting for transfers between devices  1030 us (75%)
  other arithmetic  197 us (14%)
  matrix products  64.9 us (5%)
  local copies, waits for them, and re-layouts  50.7 us (4%)
  between operations  18.7 us (1%)
    psum x7, waiting for transfers between devices, spread(): return lax.psum(jnp.where(mine, array, jnp.zeros_like(array)), axis)  672 us
    psum x2, waiting for transfers between devices, on_device(): bar_panel = lax.psum(row_source, 'col')  186 us
    psum x1, waiting for transfers between devices, on_device(): bar_factor = lax.psum(partial_value, 'row') + cot_local[diag_lr, diag_lc]  91.9 us
    psum x1, waiting for transfers between devices, on_device(): col_total = lax.psum(col_part, 'row')  78.2 us
    another operation x14, other arithmetic, on_device(): factor = jnp.linalg.cholesky(diag_block)  73.7 us
    another operation x11, other arithmetic, on_device(): pull_back = jax.vjp(jnp.linalg.cholesky, diag_block)[1]  59.6 us
    another operation x3, other arithmetic, on_device(): inverse = jax.scipy.linalg.solve_triangular(factor, identity, lower=True)  41.5 us
  transfers between devices with their start and end apart: 11, of which 11 were waited for; matrix products, arithmetic and copies ran while one was open for 6% of the time, Pallas kernels for 0%

commit v1 on v0

v1 whole, which is shorter than its diff:
```python
import jax
import jax.numpy as jnp
from jax import lax
from jax.experimental import pallas as pl
from jax.experimental.pallas import tpu as pltpu
from jax.sharding import PartitionSpec as P

W = 32
B = 256
N = 16
f32 = jnp.float32
HI = lax.Precision.HIGHEST
VMEM = pl.BlockSpec(memory_space=pltpu.VMEM)
SMEM = pl.BlockSpec(memory_space=pltpu.SMEM)
PARAMS = pltpu.CompilerParams(vmem_limit_bytes=48 * 1024 * 1024)


def dot(a,b,dims=((1,),(0,))):
    return lax.dot_general(a,b,(dims,((),())),precision=HI,preferred_element_type=f32)
def dot_nt(a,b): return dot(a,b,((1,),(1,)))
def dot_tn(a,b): return dot(a,b,((0,),(0,)))

def base_factor(tiles, sub):
    tiles=list(tiles)
    out=[None]*8
    for j in range(0,64,4):
        tj, o = j//8, j%8
        live=range(tj,8)
        C=[{t: jnp.broadcast_to(tiles[t][:, j+k:j+k+1],(8,128)) for t in live} for k in range(4)]
        R=[jnp.broadcast_to(tiles[tj][o+k:o+k+1,:],(8,128)) for k in range(4)]
        s=[[None]*4 for _ in range(4)]
        for k in range(4):
            for i in range(k,4):
                s[i][k]=jnp.broadcast_to(C[k][tj][o+i:o+i+1,:],(8,128))
        inv=[None]*4
        for k in range(4):
            inv[k]=1.0/s[k][k]
            for i in range(k+1,4):
                l=s[i][k]*inv[k]
                for m in range(i,4):
                    s[m][i]=s[m][i]-l*s[m][k]
                R[i]=R[i]-l*R[k]
                for t in live:
                    C[i][t]=C[i][t]-l*C[k][t]
        if o==0: rows=jnp.zeros((8,128),f32)
        else: rows=out[tj]
        for k in range(4):
            rows=jnp.where(sub==o+k, R[k]*lax.rsqrt(s[k][k]), rows)
        out[tj]=rows
        for t in live:
            if t==tj and o==4: continue
            upd=(C[0][t]*inv[0])*R[0]
            for k in range(1,4):
                upd=upd+(C[k][t]*inv[k])*R[k]
            new=tiles[t]-upd
            tiles[t]=jnp.where(sub>=4,new,tiles[t]) if t==tj else new
    return jnp.concatenate(out,0)

def chol_inv(a_ref, v_ref):
    sub=lax.broadcasted_iota(jnp.int32,(8,128),0)
    n,nb=256,64
    row=lax.broadcasted_iota(jnp.int32,(nb,nb),0); col=lax.broadcasted_iota(jnp.int32,(nb,nb),1)
    eye=(row==col).astype(f32)
    rr=lax.broadcasted_iota(jnp.int32,(n,n),0); cc=lax.broadcasted_iota(jnp.int32,(n,n),1)
    v_ref[...]=(rr==cc).astype(f32)
    for b in range(4):
        lo,hi=b*nb,(b+1)*nb
        d=jnp.concatenate([a_ref[lo:hi,lo:hi],eye],1)
        uw=base_factor([d[8*t:8*t+8] for t in range(8)],sub)
        u=jnp.where(row<=col,uw[:,:nb],0.0); w=uw[:,nb:]
        vp=dot(w,v_ref[lo:hi,:])
        v_ref[lo:hi,:]=vp
        a_ref[lo:hi,lo:hi]=u
        if hi<n:
            up=dot(w,a_ref[lo:hi,hi:])
            a_ref[lo:hi,hi:]=up
            a_ref[hi:,hi:]=a_ref[hi:,hi:]-dot_tn(up,up)
            v_ref[hi:,:]=v_ref[hi:,:]-dot_tn(up,vp)
    for b in range(1,4):
        a_ref[b*nb:(b+1)*nb,:b*nb]=jnp.zeros((nb,b*nb),f32)

def corner0_kernel(k_ref, v0_ref, l0_ref, p_ref, x1_ref, a_ref):
    a_ref[...] = k_ref[0]
    chol_inv(a_ref, v0_ref)
    l0_ref[...] = a_ref[...].T
    p = dot_nt(k_ref[1], v0_ref[...])
    p_ref[...] = p
    x1_ref[...] = k_ref[2] - dot_nt(p, p)


def corner1_kernel(x1_ref, v0_ref, p_ref, v1_ref, l1_ref, u_ref, a_ref):
    a_ref[...] = x1_ref[...]
    chol_inv(a_ref, v1_ref)
    l1_ref[...] = a_ref[...].T
    u_ref[...] = dot_nt(dot_tn(v0_ref[...], p_ref[...].T), v1_ref[...])


def block_shape():
    return jax.ShapeDtypeStruct((B, B), f32)


def corner0(k3):
    return pl.pallas_call(
        corner0_kernel,
        out_shape=[block_shape()] * 4,
        in_specs=[VMEM],
        out_specs=[VMEM] * 4,
        scratch_shapes=[pltpu.VMEM((B, B), f32)],
        compiler_params=PARAMS,
        name="corner0",
    )(k3)


def corner1(x1, v0, p01):
    return pl.pallas_call(
        corner1_kernel,
        out_shape=[block_shape()] * 3,
        in_specs=[VMEM] * 3,
        out_specs=[VMEM] * 3,
        scratch_shapes=[pltpu.VMEM((B, B), f32)],
        compiler_params=PARAMS,
        name="corner1",
    )(x1, v0, p01)


def partial_kernel(info, cot, r0, r1, r2, r3, other, c0, c1, c2, c3, xi, xj, row_out, col_out):
    row, col = info[0], info[1]
    sr, sc = info[2], info[3]
    mask = info[4].astype(f32)
    p, a = col // 2, col % 2
    for k, ref in enumerate((r0, r1, r2, r3)):
        for h in range(2):
            at = pl.multiple_of((p ^ (4 * h + k)) * 64, 64)
            xi[a, pl.ds(at, 64), :] = ref[64 * h : 64 * h + 64, :]
            xi[1 - a, pl.ds(at, 64), :] = other[128 * k + 64 * h : 128 * k + 64 * h + 64, :]
    for x, ref in enumerate((c0, c1, c2, c3)):
        for y in range(4):
            source = row ^ (4 * x + y)
            at = pl.multiple_of((source // 2) * 64, 64)
            xj[source % 2, pl.ds(at, 64), :] = ref[64 * y : 64 * y + 64, :]
    g00 = cot[sr, sc] * mask
    g10 = cot[sr + 1, sc]
    g11 = cot[sr + 1, sc + 1] * mask
    xi_wide = jnp.concatenate([xi[0], xi[1]], 1)
    xj_wide = jnp.concatenate([xj[0], xj[1]], 1)
    i0, i1 = xi_wide[:B], xi_wide[B:]
    j0, j1 = xj_wide[:B], xj_wide[B:]
    h_row = jnp.concatenate([dot(g00, j0), dot(g10, j0) + dot(g11, j1)], 0)
    h_col = jnp.concatenate([dot_tn(g00, i0) + dot_tn(g10, i1), dot_tn(g11, i1)], 0)
    n = dot_tn(xi_wide, h_row)
    t = n + n.T
    t3 = (t[:B, :B], t[:B, B:], t[B:, B:])
    for m in range(8):
        k, h = m % 4, m // 4
        for q in range(8):
            @pl.when((p ^ m) == q)
            def _():
                for b in range(2):
                    slot = jnp.where(a == b, 0, 1)
                    row_out[slot, k, h, :64, :] = h_row[64 * q : 64 * q + 64, B * b : B * b + B]
                    lo = 384 * b + 48 * q
                    for part in range(3):
                        at = lo + 16 * part
                        row_out[slot, k, h, 64 + 16 * part : 80 + 16 * part, :] = t3[at // B][at % B : at % B + 16]
    for target in range(16):
        m = row ^ target
        q, b = target // 2, target % 2
        col_out[m % 4, m // 4] = h_col[64 * q : 64 * q + 64, B * b : B * b + B]


def partials(info, cot, rows, other, cols):
    return pl.pallas_call(
        partial_kernel,
        out_shape=[
            jax.ShapeDtypeStruct((2, 512, B), f32),
            jax.ShapeDtypeStruct((2, 512, B), f32),
            jax.ShapeDtypeStruct((2, 4, 2, 112, B), f32),
            jax.ShapeDtypeStruct((4, 4, 64, B), f32),
        ],
        in_specs=[SMEM] + [VMEM] * 10,
        out_specs=[VMEM] * 4,
        compiler_params=PARAMS,
        name="partials",
    )(info, cot, *rows, other, *cols)


def cot_kernel(xa, xo, ca, co, info, d_out):
    first = info[1] % 2 == 0
    x0 = jnp.where(first, xa[...], xo[...])
    x1 = jnp.where(first, xo[...], xa[...])
    e0 = jnp.where(first, ca[...], co[...])
    e1 = jnp.where(first, co[...], ca[...])
    d_out[:B] = dot_tn(e0, x0)
    d_out[B : 2 * B] = dot_tn(e1, x0)
    d_out[2 * B :] = dot_tn(e1, x1)


def cot_products(info, xa, xo, ca, co):
    return pl.pallas_call(
        cot_kernel,
        out_shape=jax.ShapeDtypeStruct((3 * B, B), f32),
        in_specs=[VMEM] * 4 + [SMEM],
        out_specs=VMEM,
        compiler_params=PARAMS,
        name="cot_products",
    )(xa, xo, ca, co, info)


def factor_kernel(info, kernel, xi, xj, v0, v1, u, p01, l0, l1, out):
    row, col = info[0], info[1]
    sr, sc = info[2], info[3]
    mask = info[4].astype(f32)
    for i in range(3):
        for j in range(3):
            out[i, j] = kernel[i, j] * info[5 + 3 * i + j].astype(f32)
    w0, w1, mix = v0[...], v1[...], u[...]

    def panels(x):
        return dot_nt(x[0], w0), dot_nt(x[1], w1) - dot(x[0], mix)

    i0, i1 = panels(xi)
    j0, j1 = panels(xj)
    pi = jnp.concatenate([i0, i1], 1)
    pj = jnp.concatenate([j0, j1], 1)
    out[sr, sc] = out[sr, sc] - mask * dot_nt(pi[:B], pj[:B])
    out[sr + 1, sc] = out[sr + 1, sc] - dot_nt(pi[B:], pj[:B])
    out[sr + 1, sc + 1] = out[sr + 1, sc + 1] - mask * dot_nt(pi[B:], pj[B:])

    @pl.when(col < 2)
    def _():
        mine = jnp.where(col == 0, i0, i1)
        zero = jnp.zeros((B, B), f32)
        out[2, 0] = zero
        out[0, 0] = zero
        out[sr, 0] = mine[:B]
        out[sr + 1, 0] = mine[B:]

        @pl.when(row == 0)
        def _():
            out[0, 0] = jnp.where(col == 0, l0[...], zero)

        @pl.when(row == 1)
        def _():
            out[0, 0] = jnp.where(col == 0, p01[...], l1[...])


def factor_of(info, kernel, xi, xj, v0, v1, u, p01, l0, l1):
    return pl.pallas_call(
        factor_kernel,
        out_shape=jax.ShapeDtypeStruct((3, 3, B, B), f32),
        in_specs=[SMEM] + [VMEM] * 9,
        out_specs=VMEM,
        compiler_params=PARAMS,
        name="factor",
    )(info, kernel, xi, xj, v0, v1, u, p01, l0, l1)


def pull_cholesky(l, v, bar):
    rows = lax.broadcasted_iota(jnp.int32, (B, B), 0)
    cols = lax.broadcasted_iota(jnp.int32, (B, B), 1)
    inner = dot_tn(l, bar)
    phi = jnp.where(rows > cols, inner, jnp.where(rows == cols, 0.5 * inner, 0.0))
    full = dot(dot_tn(v, phi), v)
    return 0.5 * (full + full.T)


def grad_kernel(info, cot, mine, other, ca, co, ea, eo, v0, v1, u, p01, l0, l1, out):
    row, col = info[0], info[1]
    sr = info[2]
    keep = [[info[5 + 3 * i + j].astype(f32) for j in range(3)] for i in range(3)]
    for i in range(3):
        for j in range(3):
            out[i, j] = cot[i, j] * keep[i][j]

    @pl.when(col < 2)
    def _():
        first = col == 0
        left = jnp.where(first, mine[...], other[...])
        right = jnp.where(first, other[...], mine[...])
        h0, h1 = left[:512], right[:512]
        t = jnp.concatenate([left[512:896], right[512:896]], 0)
        d = jnp.concatenate([left[896:], right[896:]], 0)
        t00, t01, t11 = t[:B], t[B : 2 * B], t[2 * B :]
        d00, d10, d11 = d[:B], d[B : 2 * B], d[2 * B :]
        e0 = jnp.where(first, ca[...], co[...])
        e1 = jnp.where(first, co[...], ca[...])
        c10 = jnp.where(first, ea[...], eo[...])
        c11 = jnp.where(first, eo[...], ea[...])
        w0, w1, mix, p = v0[...], v1[...], u[...], p01[...]
        bar1 = e1 - dot_nt(h1, w1) + dot(h0, mix)
        g1 = dot(bar1, w1)
        g0 = dot(e0 - dot_nt(h0, w0) - dot(g1, p), w0)
        zero = jnp.zeros((B, B), f32)
        column = jnp.where(first, g0, g1)
        out[0, 0] = zero
        out[2, 0] = zero
        out[sr, 0] = column[:B] * cot_keep(info, sr)
        out[sr + 1, 0] = column[B:] * cot_keep(info, sr + 1)

        @pl.when(row < 2)
        def _():
            a10 = d10 - dot(w1, t01.T) + dot_tn(mix, t00)
            a11 = d11 - dot(w1, t11) + dot_tn(mix, t01)
            s1 = dot_nt(a11, w1) - dot(a10, mix)
            b1 = pull_cholesky(l1[...], w1, c11 - dot_tn(w1, s1))
            va = dot_tn(w1, a10)
            bar10 = c10 - 2.0 * dot(b1, p) - dot_nt(va, w0)
            s0 = dot_nt(d00 - dot(w0, t00) - dot_tn(p, va), w0)
            b0 = pull_cholesky(l0[...], w0, cot[0, 0] - dot_tn(w0, s0 + dot_tn(bar10, p)))
            g10 = dot(bar10, w0)
            upper = jnp.where(first, b0, zero)
            lower = jnp.where(first, g10, b1)
            out[0, 0] = jnp.where(row == 0, upper, lower) * keep[0][0]


def cot_keep(info, slot):
    return info[5 + 3 * slot].astype(f32)


def grad_of(info, cot, *rest):
    return pl.pallas_call(
        grad_kernel,
        out_shape=jax.ShapeDtypeStruct((3, 3, B, B), f32),
        in_specs=[SMEM] + [VMEM] * 13,
        out_specs=VMEM,
        compiler_params=PARAMS,
        name="grad",
    )(info, cot, *rest)


def flip(x, axis, m):
    return lax.ppermute(x, axis, [(i, i ^ m) for i in range(N)])


def both(pairs):
    return [(r0 * N + c0, r1 * N + c1) for (r0, c0), (r1, c1) in pairs]


def on_device(kernel, pattern, factor_cot):
    row = lax.axis_index("row")
    col = lax.axis_index("col")
    kernel3 = kernel.reshape(3, 3, B, B)
    cot3 = factor_cot.reshape(3, 3, B, B)
    row_ids = jnp.arange(3, dtype=jnp.int32) * N + row
    col_ids = jnp.arange(3, dtype=jnp.int32) * N + col
    distance = row_ids[:, None] - col_ids[None, :]
    kept = (pattern.reshape(3, 3) == 1) & (distance > 0) & (distance <= W)
    keep = ((distance == 0) | kept).astype(jnp.int32)
    sr = (row < 2).astype(jnp.int32)
    sc = (col < 2).astype(jnp.int32)
    mask = (row + N * sr >= col + N * sc).astype(jnp.int32)
    info = jnp.concatenate([jnp.stack([row, col, sr, sc, mask]), keep.reshape(9)])

    column = kernel3[:, 0] * keep[:, 0].astype(f32)[:, None, None]
    xa = lax.dynamic_slice_in_dim(column, sr, 2, 0).reshape(512, B)
    ca = lax.dynamic_slice_in_dim(cot3[:, 0], sr, 2, 0).reshape(512, B)
    corner_block = jnp.where(row < 2, column[0], 0.0)

    pieces = [
        jnp.concatenate([xa[64 * q : 64 * q + 64], corner_block[32 * q : 32 * q + 32]], 0) for q in range(8)
    ]
    row_piece = jnp.where(col < 2, pieces[0], 0.0)
    for q in range(1, 8):
        row_piece = row_piece + lax.ppermute(pieces[q], "col", [(a, 2 * q + a) for a in range(2)])
    col_piece = jnp.zeros((64, B), f32)
    for q in range(8):
        pairs = both([((s, a), (2 * q + a, s)) for s in range(N) for a in range(2)])
        col_piece = col_piece + lax.ppermute(xa[64 * q : 64 * q + 64], ("row", "col"), pairs)
    corner_piece = row_piece[64:]
    row_piece = row_piece[:64]
    zero = jnp.zeros_like(corner_piece)
    corner_piece = jnp.concatenate(
        [jnp.where(row == 0, corner_piece, zero), jnp.where(row == 1, corner_piece, zero)], 0
    )

    send = jnp.concatenate([col_piece, corner_piece], 0)
    got = [send] + [flip(send, "row", m) for m in range(1, 4)]
    corner_piece = got[0][64:] + got[1][64:] + got[2][64:] + got[3][64:]
    send = jnp.concatenate([g[:64] for g in got] + [corner_piece], 0)
    cols = [send] + [flip(send, "row", 4 * m) for m in range(1, 4)]
    corner_piece = cols[0][256:] + cols[1][256:] + cols[2][256:] + cols[3][256:]

    send = jnp.concatenate([row_piece, flip(row_piece, "col", 8)], 0)
    rows = [send] + [flip(send, "col", 2 * m) for m in range(1, 4)]
    other = flip(jnp.concatenate(rows, 0), "col", 1)

    swapped = flip(jnp.concatenate([xa, ca], 0), "col", 1)
    xo, co = swapped[:512], swapped[512:]
    d_all = cot_products(info, xa, xo, ca, co)
    d_half = lax.dynamic_slice_in_dim(d_all, 384 * (col % 2), 384, 0)
    d_piece = jnp.where(col < 2, d_half[:48], 0.0)
    for q in range(1, 8):
        d_piece = d_piece + lax.ppermute(
            d_half[48 * q : 48 * q + 48], "col", [(a, 2 * q + a) for a in range(2)]
        )
    edge = cot3[0, 0]
    from_one = lax.ppermute(edge, "row", [(1, 0)])
    ea = jnp.where(row == 0, from_one, edge)
    eo = flip(ea, "col", 1)

    xi, xj, row_out, col_out = partials(info, cot3, rows, other, cols)

    send = jnp.concatenate([corner_piece, flip(corner_piece, "col", 8)], 0).reshape(2, 2, 32, B)
    got = [send] + [flip(send, "col", 2 * m) for m in range(1, 4)]
    own = jnp.stack(got, 1).reshape(8, 2, 32, B)
    relative = jnp.arange(8, dtype=jnp.int32) ^ (col // 2)
    own = jnp.take(own, relative, axis=0).transpose(1, 0, 2, 3).reshape(2, B, B)
    across = flip(own, "col", 1)
    even = col % 2 == 0
    k3 = jnp.stack(
        [jnp.where(even, own[0], across[0]), jnp.where(even, own[1], across[1]), jnp.where(even, across[1], own[1])]
    )
    v0, l0, p01, x1 = corner0(k3)
    v1, l1, u = corner1(x1, v0, p01)

    part = row_out[0] + flip(row_out[1], "col", 1)
    part = part[0] + flip(part[1], "col", 2) + flip(part[2], "col", 4) + flip(part[3], "col", 6)
    part = part[0] + flip(part[1], "col", 8)
    td = jnp.concatenate([part[64:], d_piece], 0)
    td = td + flip(td, "row", 1) + flip(td, "row", 2) + flip(td, "row", 3)
    td = td + flip(td, "row", 4) + flip(td, "row", 8) + flip(td, "row", 12)
    cpart = col_out[0] + flip(col_out[1], "row", 1) + flip(col_out[2], "row", 2) + flip(col_out[3], "row", 3)
    cpart = cpart[0] + flip(cpart[1], "row", 4) + flip(cpart[2], "row", 8) + flip(cpart[3], "row", 12)

    send = jnp.concatenate([part[:64], td], 0)
    by_row = [send] + [
        lax.ppermute(send, "col", [(2 * q + a, a) for a in range(2)]) for q in range(1, 8)
    ]
    by_col = [
        lax.ppermute(cpart, ("row", "col"), both([((2 * q + b, s), (s, b)) for s in range(N) for b in range(2)]))
        for q in range(8)
    ]
    mine = jnp.concatenate(
        [by_row[q][:64] + by_col[q] for q in range(8)]
        + [by_row[q][64:112] for q in range(8)]
        + [by_row[q][112:] for q in range(8)],
        0,
    )
    theirs = flip(mine, "col", 1)

    factor_out = factor_of(info, kernel3, xi, xj, v0, v1, u, p01, l0, l1)
    grad_out = grad_of(info, cot3, mine, theirs, ca, co, ea, eo, v0, v1, u, p01, l0, l1)
    return (factor_out.reshape(kernel.shape), grad_out.reshape(kernel.shape))


def solution(mesh):
    spec = P(None, "row", None, "col", None, None)
    return jax.shard_map(
        on_device,
        mesh=mesh,
        in_specs=(spec, P(None, "row", None, "col"), spec),
        out_specs=(spec, spec),
        check_vma=False,
    )
```

time: 1380 us -> 428 us (0.31)
  waiting for transfers between devices: 1030 us -> 93.9 us
  starting transfers between devices: 1.24 us -> 247 us
  other arithmetic: 197 us -> 6.22 us
  matrix products: 64.9 us -> 0 us
  Pallas kernels: 0 us -> 61.3 us
  local copies, waits for them, and re-layouts: 50.7 us -> 9.22 us
  between operations: 18.7 us -> 2.24 us
    psum x11 -> x0, waiting for transfers between devices: 1030 us -> none  [the longest x7 672 us: spread(): return lax.psum(jnp.where(mine, array, jnp.zeros_like(array)), axis)]
    ppermute x0 -> x74, starting transfers between devices: none -> 247 us  [the longest x8 95.7 us: on_device(): lax.ppermute(cpart, ('row', 'col'), both([((2 * q + b, s), (s, b)) for s...]
    another operation x28 -> x2, other arithmetic: 175 us -> 0.09 us  [the longest x1 0.05 us: on_device(): jnp.stack([jnp.where(even, own[0], across[0]), jnp.where(even, own[1], ac...]
    ppermute x0 -> x74, waiting for transfers between devices: none -> 93.9 us  [the longest x36 49.8 us: flip(): return lax.ppermute(x, axis, [(i, i ^ m) for i in range(N)])]
    pallas_call x0 -> x6, Pallas kernels: none -> 61.3 us  [the longest x1 15 us: grad_of(): pl.pallas_call(grad_kernel, out_shape=jax.ShapeDtypeStruct((3, 3, B, B),...]
    dot_general x14 -> x0, matrix products: 46 us -> none  [the longest x2 10.8 us: on_device(): jnp.einsum('abji,ajk->bik', masked, row_panel, precision=highest)]
    another operation x40 -> x0, local copies, waits for them, and re-layouts: 30.9 us -> none  [the longest x12 13 us: on_device(): pull_back = jax.vjp(jnp.linalg.cholesky, diag_block)[1]]
    another operation x24 -> x0, matrix products: 18.9 us -> none  [the longest x14 10.5 us: on_device(): pull_back = jax.vjp(jnp.linalg.cholesky, diag_block)[1]]
  transfers between devices with their start and end apart: 11 -> 74, of which waited for: 11 -> 22; matrix products, arithmetic and copies ran while one was open for 6% -> 3% of each run, Pallas kernels for 0% -> 11%
where the time goes in v1:
time: 428 us; the launch traced here: 420 us
  starting transfers between devices  247 us (58%)
  waiting for transfers between devices  93.9 us (22%)
  Pallas kernels  61.3 us (14%)
  local copies, waits for them, and re-layouts  9.22 us (2%)
  other arithmetic  6.22 us (1%)
    ppermute x8, starting transfers between devices, on_device(): lax.ppermute(cpart, ('row', 'col'), both([((2 * q + b, s), (s, b)) for s...  95.7 us
    ppermute x36, starting transfers between devices, flip(): return lax.ppermute(x, axis, [(i, i ^ m) for i in range(N)])  82.6 us
    ppermute x36, waiting for transfers between devices, flip(): return lax.ppermute(x, axis, [(i, i ^ m) for i in range(N)])  49.8 us
    ppermute x8, waiting for transfers between devices, on_device(): lax.ppermute(cpart, ('row', 'col'), both([((2 * q + b, s), (s, b)) for s...  43.2 us
    ppermute x8, starting transfers between devices, on_device(): lax.ppermute(xa[64 * q:64 * q + 64], ('row', 'col'), pairs)  25.2 us
    ppermute x7, starting transfers between devices, on_device(): lax.ppermute(d_half[48 * q:48 * q + 48], 'col', [(a, 2 * q + a) for a in...  24.6 us
    pallas_call x1, Pallas kernels, grad_of(): pl.pallas_call(grad_kernel, out_shape=jax.ShapeDtypeStruct((3, 3, B, B),...  15 us
    pallas_call x1, Pallas kernels, corner0(): pl.pallas_call(corner0_kernel, out_shape=[block_shape()] * 4, in_specs=[V...  14.6 us
  transfers between devices with their start and end apart: 74, of which 22 were waited for; matrix products, arithmetic and copies ran while one was open for 3% of the time, Pallas kernels for 11%

profile of v1, /device:TPU:1, one launch (start us, length us, event | category | flops | bytes accessed | tf_op | source)
XLA Modules:
  0.0 420.3 jit_solution(8634526201673181978)
XLA Ops:
  1.6 1.9 copy.21
  4.6 4.6 %collective-permute-start.12 = (f32[64,256]{1,0:T(8,128)S(1)}, f32[64,256]{1,0:T(8,128)S(1)}, u32[]{:S(2)}, u32[]{:S(2)}) collective-permute-start(f32[64,256]{1,0:T(8,128)S(1)} %get-tuple-element.56), channel_id=1, source_target_pairs={{0,0},{1,16},{16,1},{17,17},{32,2},{33,18},{48,3},{49,19},{64,4},{... | collective-permute-start | bytes 196616 | tf_op jit(solution)/shard_map/ppermute | solution.py:368
  9.2 4.4 %collective-permute-start.13 = (f32[64,256]{1,0:T(8,128)S(1)}, f32[64,256]{1,0:T(8,128)S(1)}, u32[]{:S(2)}, u32[]{:S(2)}) collective-permute-start(f32[64,256]{1,0:T(8,128)S(1)} %get-tuple-element.63), channel_id=1, source_target_pairs={{0,32},{1,48},{16,33},{17,49},{32,34},{33,50},{48,35},{49,51},{64,... | collective-permute-start | bytes 196616 | tf_op jit(solution)/shard_map/ppermute | solution.py:368
  13.5 2.8 collective-permute-start.14
  16.4 4.0 collective-permute-start.15
  20.4 5.3 %collective-permute-start.16 = (f32[64,256]{1,0:T(8,128)S(1)}, f32[64,256]{1,0:T(8,128)}, u32[]{:S(2)}, u32[]{:S(2)}) collective-permute-start(f32[64,256]{1,0:T(8,128)S(1)} %get-tuple-element.60), channel_id=1, source_target_pairs={{0,128},{1,144},{16,129},{17,145},{32,130},{33,146},{48,131},{49,1... | collective-permute-start | bytes 196616 | tf_op jit(solution)/shard_map/ppermute | solution.py:368
  28.6 1.6 collective-permute-start.17
  45.3 2.8 collective-permute-start.7
  48.0 1.8 collective-permute-start.20
  49.9 2.5 collective-permute-start.22
  52.6 3.7 collective-permute-start.9
  56.3 2.4 collective-permute-start.10
  60.1 3.3 collective-permute-done.10.r3
  63.3 4.5 %collective-permute-start.11 = (f32[512,256]{1,0:T(8,128)S(1)}, f32[512,256]{1,0:T(8,128)S(1)}, u32[]{:S(2)}, u32[]{:S(2)}) collective-permute-start(f32[512,256]{1,0:T(8,128)S(1)} %constant_dynamic-update-slice_fusion), channel_id=1, source_target_pairs={{0,1},{1,0},{2,3},{3,2},{4,5},{5,4},{6,7},{7,6},{8,9},{9,8},{10,11... | collective-permute-start | bytes 1572872 | tf_op jit(solution)/shard_map/ppermute | solution.py:332
  68.0 2.9 collective-permute-start.24
  72.1 1.7 slice_bitcast_fusion.2
  73.7 3.6 collective-permute-done.23.c1
  77.3 8.5 %collective-permute-done.24.c2 = f32[320,256]{1,0:T(8,128)S(1)} collective-permute-done((f32[320,256]{1,0:T(8,128)S(1)}, f32[320,256]{1,0:T(8,128)S(1)}, u32[]{:S(2)}, u32[]{:S(2)}) %collective-permute-start.24) | collective-permute-done | bytes 327712 | tf_op jit(solution)/shard_map/ppermute | solution.py:332
  85.8 2.2 collective-permute-done.25.c3
  88.0 8.3 %partials.1 = (f32[2,512,256]{2,1,0:T(8,128)S(1)}, f32[2,512,256]{2,1,0:T(8,128)S(1)}, f32[2,4,2,112,256]{4,3,2,1,0:T(8,128)}, f32[4,4,64,256]{3,2,1,0:T(8,128)S(1)}) custom-call(s32[14]{0:T(128)S(1)} %concatenate.59.info, f32[3,3,256,256]{3,2,1,0:T(8,128)} %bitcast.126, f32[128,256]{1,0:T(8,128)S(1)} %pad_maximum_fusion.4.r0, ...), custom_call_target="tpu_custom_call" | custom-call | tf_op jit(solution)/shard_map/partials/pallas_call | solution.py:172
  96.3 1.9 slice_bitcast_fusion
  100.1 2.8 collective-permute-start.37
  103.9 2.2 cot_products.1
  106.2 3.7 collective-permute-start.44
  109.9 2.5 collective-permute-start.45
  112.4 2.7 collective-permute-done.37
  115.1 2.0 collective-permute-done.38
  117.3 1.7 collective-permute-start.32
  121.8 4.2 %collective-permute-done.32 = f32[2,112,256]{2,1,0:T(8,128)S(1)} collective-permute-done((f32[2,112,256]{2,1,0:T(8,128)S(1)}, f32[2,112,256]{2,1,0:T(8,128)S(1)}, u32[]{:S(2)}, u32[]{:S(2)}) %collective-permute-start.32) | collective-permute-done | bytes 229408 | tf_op jit(solution)/shard_map/ppermute | solution.py:332
  126.0 3.0 collective-permute-start.46
  129.0 3.4 collective-permute-start.47
  132.5 2.8 collective-permute-done.34
  135.3 9.4 %collective-permute-start.48 = (f32[48,256]{1,0:T(8,128)S(1)}, f32[48,256]{1,0:T(8,128)S(1)}, u32[]{:S(2)}, u32[]{:S(2)}) collective-permute-start(f32[48,256]{1,0:T(8,128)S(1)} %get-tuple-element.46), channel_id=1, source_target_pairs={{0,10},{1,11},{16,26},{17,27},{32,42},{33,43},{48,58},{49,59},{64,... | collective-permute-start | bytes 147464 | tf_op jit(solution)/shard_map/ppermute | solution.py:393
  150.3 14.2 %collective-permute-start.35 = (f32[112,256]{1,0:T(8,128)S(1)}, f32[112,256]{1,0:T(8,128)S(1)}, u32[]{:S(2)}, u32[]{:S(2)}) collective-permute-start(f32[112,256]{1,0:T(8,128)S(1)} %slice_bitcast_fusion.10), channel_id=1, source_target_pairs={{0,8},{1,9},{2,10},{3,11},{4,12},{5,13},{6,14},{7,15},{8,0},{9,1},... | collective-permute-start | bytes 344072 | tf_op jit(solution)/shard_map/ppermute | solution.py:332
  164.5 12.1 %collective-permute-done.35 = f32[112,256]{1,0:T(8,128)S(1)} collective-permute-done((f32[112,256]{1,0:T(8,128)S(1)}, f32[112,256]{1,0:T(8,128)S(1)}, u32[]{:S(2)}, u32[]{:S(2)}) %collective-permute-start.35) | collective-permute-done | bytes 114720 | tf_op jit(solution)/shard_map/ppermute | solution.py:332
  176.6 2.3 collective-permute-start.41
  180.3 2.5 collective-permute-start.52
  183.4 4.5 %collective-permute-start.42 = (f32[64,256]{1,0:T(8,128)S(1)}, f32[64,256]{1,0:T(8,128)S(1)}, u32[]{:S(2)}, u32[]{:S(2)}) collective-permute-start(f32[64,256]{1,0:T(8,128)S(1)} %fusion.16), channel_id=1, source_target_pairs={{0,0},{16,1},{1,16},{17,17},{2,32},{18,33},{3,48},{19,49},{4,64},{... | collective-permute-start | bytes 196616 | tf_op jit(solution)/shard_map/ppermute | solution.py:430
  188.6 1.6 collective-permute-start.55
  190.2 8.1 %collective-permute-start.56 = (f32[96,256]{1,0:T(8,128)S(1)}, f32[96,256]{1,0:T(8,128)S(1)}, u32[]{:S(2)}, u32[]{:S(2)}) collective-permute-start(f32[96,256]{1,0:T(8,128)S(1)} %add_add_fusion.1), channel_id=1, source_target_pairs={{0,192},{16,208},{32,224},{48,240},{64,128},{80,144},{96,160},{112... | collective-permute-start | bytes 294920 | tf_op jit(solution)/shard_map/ppermute | solution.py:332
  198.4 2.0 collective-permute-done.56
  201.7 12.6 %collective-permute-start.58 = (f32[64,256]{1,0:T(8,128)S(1)}, f32[64,256]{1,0:T(8,128)S(1)}, u32[]{:S(2)}, u32[]{:S(2)}) collective-permute-start(f32[64,256]{1,0:T(8,128)S(1)} %fusion.16), channel_id=1, source_target_pairs={{32,0},{48,1},{33,16},{49,17},{34,32},{50,33},{35,48},{51,49},{36,... | collective-permute-start | bytes 196616 | tf_op jit(solution)/shard_map/ppermute | solution.py:430
  214.3 1.6 collective-permute-start.27
  215.9 2.6 collective-permute-start.28
  218.5 1.9 collective-permute-done.58
  220.5 13.7 %collective-permute-start.60 = (f32[64,256]{1,0:T(8,128)S(1)}, f32[64,256]{1,0:T(8,128)S(1)}, u32[]{:S(2)}, u32[]{:S(2)}) collective-permute-start(f32[64,256]{1,0:T(8,128)S(1)} %fusion.16), channel_id=1, source_target_pairs={{64,0},{80,1},{65,16},{81,17},{66,32},{82,33},{67,48},{83,49},{68,... | collective-permute-start | bytes 196616 | tf_op jit(solution)/shard_map/ppermute | solution.py:430
  235.5 5.2 %collective-permute-done.60 = f32[64,256]{1,0:T(8,128)S(1)} collective-permute-done((f32[64,256]{1,0:T(8,128)S(1)}, f32[64,256]{1,0:T(8,128)S(1)}, u32[]{:S(2)}, u32[]{:S(2)}) %collective-permute-start.60) | collective-permute-done | bytes 65568 | tf_op jit(solution)/shard_map/ppermute | solution.py:430
  240.6 13.0 %collective-permute-start.62 = (f32[64,256]{1,0:T(8,128)S(1)}, f32[64,256]{1,0:T(8,128)S(1)}, u32[]{:S(2)}, u32[]{:S(2)}) collective-permute-start(f32[64,256]{1,0:T(8,128)S(1)} %fusion.16), channel_id=1, source_target_pairs={{96,0},{112,1},{97,16},{113,17},{98,32},{114,33},{99,48},{115,49},... | collective-permute-start | bytes 196616 | tf_op jit(solution)/shard_map/ppermute | solution.py:430
  254.9 6.8 %collective-permute-done.62 = f32[64,256]{1,0:T(8,128)S(1)} collective-permute-done((f32[64,256]{1,0:T(8,128)S(1)}, f32[64,256]{1,0:T(8,128)S(1)}, u32[]{:S(2)}, u32[]{:S(2)}) %collective-permute-start.62) | collective-permute-done | bytes 65568 | tf_op jit(solution)/shard_map/ppermute | solution.py:430
  261.7 11.2 %collective-permute-start.64 = (f32[64,256]{1,0:T(8,128)S(1)}, f32[64,256]{1,0:T(8,128)S(1)}, u32[]{:S(2)}, u32[]{:S(2)}) collective-permute-start(f32[64,256]{1,0:T(8,128)S(1)} %fusion.16), channel_id=1, source_target_pairs={{128,0},{144,1},{129,16},{145,17},{130,32},{146,33},{131,48},{147,... | collective-permute-start | bytes 196616 | tf_op jit(solution)/shard_map/ppermute | solution.py:430
  274.2 6.7 %collective-permute-done.64 = f32[64,256]{1,0:T(8,128)S(1)} collective-permute-done((f32[64,256]{1,0:T(8,128)S(1)}, f32[64,256]{1,0:T(8,128)S(1)}, u32[]{:S(2)}, u32[]{:S(2)}) %collective-permute-start.64) | collective-permute-done | bytes 65568 | tf_op jit(solution)/shard_map/ppermute | solution.py:430
  280.8 14.2 %collective-permute-start.66 = (f32[64,256]{1,0:T(8,128)S(1)}, f32[64,256]{1,0:T(8,128)S(1)}, u32[]{:S(2)}, u32[]{:S(2)}) collective-permute-start(f32[64,256]{1,0:T(8,128)S(1)} %fusion.16), channel_id=1, source_target_pairs={{160,0},{176,1},{161,16},{177,17},{162,32},{178,33},{163,48},{179,... | collective-permute-start | bytes 196616 | tf_op jit(solution)/shard_map/ppermute | solution.py:430
  296.4 8.3 %collective-permute-done.66 = f32[64,256]{1,0:T(8,128)S(1)} collective-permute-done((f32[64,256]{1,0:T(8,128)S(1)}, f32[64,256]{1,0:T(8,128)S(1)}, u32[]{:S(2)}, u32[]{:S(2)}) %collective-permute-start.66) | collective-permute-done | bytes 65568 | tf_op jit(solution)/shard_map/ppermute | solution.py:430
  304.6 12.4 %collective-permute-start.68 = (f32[64,256]{1,0:T(8,128)S(1)}, f32[64,256]{1,0:T(8,128)S(1)}, u32[]{:S(2)}, u32[]{:S(2)}) collective-permute-start(f32[64,256]{1,0:T(8,128)S(1)} %fusion.16), channel_id=1, source_target_pairs={{192,0},{208,1},{193,16},{209,17},{194,32},{210,33},{195,48},{211,... | collective-permute-start | bytes 196616 | tf_op jit(solution)/shard_map/ppermute | solution.py:430
  318.4 6.4 %collective-permute-done.68 = f32[64,256]{1,0:T(8,128)S(1)} collective-permute-done((f32[64,256]{1,0:T(8,128)S(1)}, f32[64,256]{1,0:T(8,128)S(1)}, u32[]{:S(2)}, u32[]{:S(2)}) %collective-permute-start.68) | collective-permute-done | bytes 65568 | tf_op jit(solution)/shard_map/ppermute | solution.py:430
  324.7 14.2 %collective-permute-start.70 = (f32[64,256]{1,0:T(8,128)S(1)}, f32[64,256]{1,0:T(8,128)S(1)}, u32[]{:S(2)}, u32[]{:S(2)}) collective-permute-start(f32[64,256]{1,0:T(8,128)S(1)} %fusion.16), channel_id=1, source_target_pairs={{224,0},{240,1},{225,16},{241,17},{226,32},{242,33},{227,48},{243,... | collective-permute-start | bytes 196616 | tf_op jit(solution)/shard_map/ppermute | solution.py:430
  340.3 8.0 %collective-permute-done.70 = f32[64,256]{1,0:T(8,128)S(1)} collective-permute-done((f32[64,256]{1,0:T(8,128)S(1)}, f32[64,256]{1,0:T(8,128)S(1)}, u32[]{:S(2)}, u32[]{:S(2)}) %collective-permute-start.70) | collective-permute-done | bytes 65568 | tf_op jit(solution)/shard_map/ppermute | solution.py:430
  350.1 4.4 %collective-permute-done.29 = f32[2,2,32,256]{3,2,1,0:T(8,128)S(1)} collective-permute-done((f32[2,2,32,256]{3,2,1,0:T(8,128)S(1)}, f32[2,2,32,256]{3,2,1,0:T(8,128)S(1)}, u32[]{:S(2)}, u32[]{:S(2)}) %collective-permute-start.29) | collective-permute-done | bytes 131104 | tf_op jit(solution)/shard_map/ppermute | solution.py:332
  355.3 1.6 collective-permute-start.30
  357.9 9.9 %collective-permute-start.73 = (f32[256,256]{1,0:T(8,128)S(1)}, f32[256,256]{1,0:T(8,128)S(1)}, u32[]{:S(2)}, u32[]{:S(2)}) collective-permute-start(f32[256,256]{1,0:T(8,128)S(1)} %broadcast_select_fusion.ea), channel_id=1, source_target_pairs={{0,1},{1,0},{2,3},{3,2},{4,5},{5,4},{6,7},{7,6},{8,9},{9,8},{10,11... | collective-permute-start | bytes 786440 | tf_op jit(solution)/shard_map/ppermute | solution.py:332
  369.2 14.6 %corner0.1 = (f32[256,256]{1,0:T(8,128)S(1)}, f32[256,256]{1,0:T(8,128)S(1)}, f32[256,256]{1,0:T(8,128)S(1)}, f32[256,256]{1,0:T(8,128)S(1)}) custom-call(f32[3,256,256]{2,1,0:T(8,128)S(1)} %pad_maximum_fusion.1.k_ref), custom_call_target="tpu_custom_call" | custom-call | tf_op jit(solution)/shard_map/corner0/pallas_call | solution.py:103
  383.8 14.3 %corner1.1 = (f32[256,256]{1,0:T(8,128)S(1)}, f32[256,256]{1,0:T(8,128)S(1)}, f32[256,256]{1,0:T(8,128)S(1)}) custom-call(f32[256,256]{1,0:T(8,128)S(1)} %get-tuple-element.16.x1_ref, f32[256,256]{1,0:T(8,128)S(1)} %get-tuple-element.15.v0_ref.v0, f32[256,256]{1,0:T(8,128)S(1)} %get-tuple-element.17.p_ref.p01), custom_call_target="tpu_custom_call" | custom-call | tf_op jit(solution)/shard_map/corner1/pallas_call | solution.py:115
  398.1 6.8 %factor.1 = f32[3,3,256,256]{3,2,1,0:T(8,128)} custom-call(s32[14]{0:T(128)S(1)} %concatenate.59.info, f32[3,3,256,256]{3,2,1,0:T(8,128)S(1)} %bitcast.117, f32[2,512,256]{2,1,0:T(8,128)S(1)} %copy-done.2, f32[2,512,256]{2,1,0:T(8,128)S(1)} %copy-done.4, f32[256,256]{1,0:T(8,128)S(1)} %get-tuple-element.15.v0_ref.v0, f32[256,256]{1,0:T(8,128)S(1)} %get-tuple-element.18.v1, ...), custom_call_target="tpu_custom_call" | custom-call | tf_op jit(solution)/shard_map/factor/pallas_call | solution.py:248
  404.9 15.0 %grad.1 = f32[3,3,256,256]{3,2,1,0:T(8,128)} custom-call(s32[14]{0:T(128)S(1)} %concatenate.59.info, f32[3,3,256,256]{3,2,1,0:T(8,128)} %bitcast.128, f32[1280,256]{1,0:T(8,128)S(1)} %constant_dynamic-update-slice_fusion.10.mine, f32[1280,256]{1,0:T(8,128)} %collective-permute-done.71.other, f32[512,256]{1,0:T(8,128)S(1)} %bitcast.123, ...), custom_call_target="tpu_custom_call" | custom-call | tf_op jit(solution)/shard_map/grad/pallas_call | solution.py:321
  (201 shorter events, 50.7 us)
Async XLA Ops:
  4.6 24.0 %collective-permute-start.12 = (f32[64,256]{1,0:T(8,128)S(1)}, f32[64,256]{1,0:T(8,128)S(1)}, u32[]{:S(2)}, u32[]{:S(2)}) collective-permute-start(f32[64,256]{1,0:T(8,128)S(1)} %get-tuple-element.56), channel_id=1, source_target_pairs={{0,0},{1,16},{16,1},{17,17},{32,2},{33,18},{48,3},{49,19},{64,4},{... | collective-permute-start | bytes 196616 | tf_op jit(solution)/shard_map/ppermute | solution.py:368
  9.2 20.9 %collective-permute-start.13 = (f32[64,256]{1,0:T(8,128)S(1)}, f32[64,256]{1,0:T(8,128)S(1)}, u32[]{:S(2)}, u32[]{:S(2)}) collective-permute-start(f32[64,256]{1,0:T(8,128)S(1)} %get-tuple-element.63), channel_id=1, source_target_pairs={{0,32},{1,48},{16,33},{17,49},{32,34},{33,50},{48,35},{49,51},{64,... | collective-permute-start | bytes 196616 | tf_op jit(solution)/shard_map/ppermute | solution.py:368
  13.5 17.9 %collective-permute-start.14 = (f32[64,256]{1,0:T(8,128)S(1)}, f32[64,256]{1,0:T(8,128)S(1)}, u32[]{:S(2)}, u32[]{:S(2)}) collective-permute-start(f32[64,256]{1,0:T(8,128)S(1)} %get-tuple-element.62), channel_id=1, source_target_pairs={{0,64},{1,80},{16,65},{17,81},{32,66},{33,82},{48,67},{49,83},{64,... | collective-permute-start | bytes 196616 | tf_op jit(solution)/shard_map/ppermute | solution.py:368
  16.4 16.4 %collective-permute-start.15 = (f32[64,256]{1,0:T(8,128)S(1)}, f32[64,256]{1,0:T(8,128)}, u32[]{:S(2)}, u32[]{:S(2)}) collective-permute-start(f32[64,256]{1,0:T(8,128)S(1)} %get-tuple-element.61), channel_id=1, source_target_pairs={{0,96},{1,112},{16,97},{17,113},{32,98},{33,114},{48,99},{49,115},... | collective-permute-start | bytes 196616 | tf_op jit(solution)/shard_map/ppermute | solution.py:368
  20.4 13.7 %collective-permute-start.16 = (f32[64,256]{1,0:T(8,128)S(1)}, f32[64,256]{1,0:T(8,128)}, u32[]{:S(2)}, u32[]{:S(2)}) collective-permute-start(f32[64,256]{1,0:T(8,128)S(1)} %get-tuple-element.60), channel_id=1, source_target_pairs={{0,128},{1,144},{16,129},{17,145},{32,130},{33,146},{48,131},{49,1... | collective-permute-start | bytes 196616 | tf_op jit(solution)/shard_map/ppermute | solution.py:368
  28.6 6.8 %collective-permute-start.17 = (f32[64,256]{1,0:T(8,128)S(1)}, f32[64,256]{1,0:T(8,128)S(1)}, u32[]{:S(2)}, u32[]{:S(2)}) collective-permute-start(f32[64,256]{1,0:T(8,128)S(1)} %get-tuple-element.59), channel_id=1, source_target_pairs={{0,160},{1,176},{16,161},{17,177},{32,162},{33,178},{48,163},{49,1... | collective-permute-start | bytes 196616 | tf_op jit(solution)/shard_map/ppermute | solution.py:368
  30.1 6.6 %collective-permute-start.18 = (f32[64,256]{1,0:T(8,128)S(1)}, f32[64,256]{1,0:T(8,128)S(1)}, u32[]{:S(2)}, u32[]{:S(2)}) collective-permute-start(f32[64,256]{1,0:T(8,128)S(1)} %get-tuple-element.58), channel_id=1, source_target_pairs={{0,192},{1,208},{16,193},{17,209},{32,194},{33,210},{48,195},{49,2... | collective-permute-start | bytes 196616 | tf_op jit(solution)/shard_map/ppermute | solution.py:368
  31.4 6.6 %collective-permute-start.19 = (f32[64,256]{1,0:T(8,128)S(1)}, f32[64,256]{1,0:T(8,128)S(1)}, u32[]{:S(2)}, u32[]{:S(2)}) collective-permute-start(f32[64,256]{1,0:T(8,128)S(1)} %get-tuple-element.57), channel_id=1, source_target_pairs={{0,224},{1,240},{16,225},{17,241},{32,226},{33,242},{48,227},{49,2... | collective-permute-start | bytes 196616 | tf_op jit(solution)/shard_map/ppermute | solution.py:368
  32.8 6.6 %collective-permute-start = (f32[96,256]{1,0:T(8,128)S(1)}, f32[96,256]{1,0:T(8,128)S(1)}, u32[]{:S(2)}, u32[]{:S(2)}) collective-permute-start(f32[96,256]{1,0:T(8,128)S(1)} %pad_maximum_fusion.7), channel_id=1, source_target_pairs={{0,2},{1,3},{16,18},{17,19},{32,34},{33,35},{48,50},{49,51},{64,66... | collective-permute-start | bytes 294920 | tf_op jit(solution)/shard_map/ppermute | solution.py:364
  34.1 6.6 %collective-permute-start.1 = (f32[96,256]{1,0:T(8,128)S(1)}, f32[96,256]{1,0:T(8,128)S(1)}, u32[]{:S(2)}, u32[]{:S(2)}) collective-permute-start(f32[96,256]{1,0:T(8,128)S(1)} %pad_maximum_fusion.8), channel_id=1, source_target_pairs={{0,4},{1,5},{16,20},{17,21},{32,36},{33,37},{48,52},{49,53},{64,68... | collective-permute-start | bytes 294920 | tf_op jit(solution)/shard_map/ppermute | solution.py:364
  35.4 7.5 %collective-permute-start.2 = (f32[96,256]{1,0:T(8,128)S(1)}, f32[96,256]{1,0:T(8,128)S(1)}, u32[]{:S(2)}, u32[]{:S(2)}) collective-permute-start(f32[96,256]{1,0:T(8,128)S(1)} %pad_maximum_fusion.9), channel_id=1, source_target_pairs={{0,6},{1,7},{16,22},{17,23},{32,38},{33,39},{48,54},{49,55},{64,70... | collective-permute-start | bytes 294920 | tf_op jit(solution)/shard_map/ppermute | solution.py:364
  36.7 7.6 %collective-permute-start.3 = (f32[96,256]{1,0:T(8,128)S(1)}, f32[96,256]{1,0:T(8,128)S(1)}, u32[]{:S(2)}, u32[]{:S(2)}) collective-permute-start(f32[96,256]{1,0:T(8,128)S(1)} %pad_maximum_fusion.10), channel_id=1, source_target_pairs={{0,8},{1,9},{16,24},{17,25},{32,40},{33,41},{48,56},{49,57},{64,72... | collective-permute-start | bytes 294920 | tf_op jit(solution)/shard_map/ppermute | solution.py:364
  42.9 60.9 %collective-permute-start.43 = (f32[1024,256]{1,0:T(8,128)S(1)}, f32[1024,256]{1,0:T(8,128)S(1)}, u32[]{:S(2)}, u32[]{:S(2)}) collective-permute-start(f32[1024,256]{1,0:T(8,128)S(1)} %pad_maximum_fusion), channel_id=1, source_target_pairs={{0,1},{1,0},{2,3},{3,2},{4,5},{5,4},{6,7},{7,6},{8,9},{9,8},{10,11... | collective-permute-start | bytes 3145736 | tf_op jit(solution)/shard_map/ppermute | solution.py:332
  45.3 7.2 %collective-permute-start.7 = (f32[64,256]{1,0:T(8,128)S(1)}, f32[64,256]{1,0:T(8,128)S(1)}, u32[]{:S(2)}, u32[]{:S(2)}) collective-permute-start(f32[64,256]{1,0:T(8,128)S(1)} %get-tuple-element.80), channel_id=1, source_target_pairs={{0,8},{1,9},{2,10},{3,11},{4,12},{5,13},{6,14},{7,15},{8,0},{9,1},... | collective-permute-start | bytes 196616 | tf_op jit(solution)/shard_map/ppermute | solution.py:332
  49.9 6.4 %collective-permute-start.21 = (f32[128,256]{1,0:T(8,128)S(1)}, f32[128,256]{1,0:T(8,128)S(1)}, u32[]{:S(2)}, u32[]{:S(2)}) collective-permute-start(f32[128,256]{1,0:T(8,128)S(1)} %pad_maximum_fusion.5), channel_id=1, source_target_pairs={{0,32},{16,48},{32,0},{48,16},{64,96},{80,112},{96,64},{112,80},{1... | collective-permute-start | bytes 393224 | tf_op jit(solution)/shard_map/ppermute | solution.py:332
  49.9 8.9 %collective-permute-start.22 = (f32[128,256]{1,0:T(8,128)S(1)}, f32[128,256]{1,0:T(8,128)S(1)}, u32[]{:S(2)}, u32[]{:S(2)}) collective-permute-start(f32[128,256]{1,0:T(8,128)S(1)} %pad_maximum_fusion.5), channel_id=1, source_target_pairs={{0,48},{16,32},{32,16},{48,0},{64,112},{80,96},{96,80},{112,64},{1... | collective-permute-start | bytes 393224 | tf_op jit(solution)/shard_map/ppermute | solution.py:332
  52.5 6.3 %collective-permute-start.8 = (f32[128,256]{1,0:T(8,128)S(1)}, f32[128,256]{1,0:T(8,128)S(1)}, u32[]{:S(2)}, u32[]{:S(2)}) collective-permute-start(f32[128,256]{1,0:T(8,128)S(1)} %pad_maximum_fusion.4.r0), channel_id=1, source_target_pairs={{0,2},{1,3},{2,0},{3,1},{4,6},{5,7},{6,4},{7,5},{8,10},{9,11},{10,... | collective-permute-start | bytes 393224 | tf_op jit(solution)/shard_map/ppermute | solution.py:332
  52.6 7.5 %collective-permute-start.9 = (f32[128,256]{1,0:T(8,128)S(1)}, f32[128,256]{1,0:T(8,128)S(1)}, u32[]{:S(2)}, u32[]{:S(2)}) collective-permute-start(f32[128,256]{1,0:T(8,128)S(1)} %pad_maximum_fusion.4.r0), channel_id=1, source_target_pairs={{0,4},{1,5},{2,6},{3,7},{4,0},{5,1},{6,2},{7,3},{8,12},{9,13},{10,... | collective-permute-start | bytes 393224 | tf_op jit(solution)/shard_map/ppermute | solution.py:332
  56.3 7.0 %collective-permute-start.10 = (f32[128,256]{1,0:T(8,128)S(1)}, f32[128,256]{1,0:T(8,128)S(1)}, u32[]{:S(2)}, u32[]{:S(2)}) collective-permute-start(f32[128,256]{1,0:T(8,128)S(1)} %pad_maximum_fusion.4.r0), channel_id=1, source_target_pairs={{0,6},{1,7},{2,4},{3,5},{4,2},{5,3},{6,0},{7,1},{8,14},{9,15},{10,... | collective-permute-start | bytes 393224 | tf_op jit(solution)/shard_map/ppermute | solution.py:332
  63.3 24.6 %collective-permute-start.11 = (f32[512,256]{1,0:T(8,128)S(1)}, f32[512,256]{1,0:T(8,128)S(1)}, u32[]{:S(2)}, u32[]{:S(2)}) collective-permute-start(f32[512,256]{1,0:T(8,128)S(1)} %constant_dynamic-update-slice_fusion), channel_id=1, source_target_pairs={{0,1},{1,0},{2,3},{3,2},{4,5},{5,4},{6,7},{7,6},{8,9},{9,8},{10,11... | collective-permute-start | bytes 1572872 | tf_op jit(solution)/shard_map/ppermute | solution.py:332
  67.9 9.4 %collective-permute-start.23 = (f32[320,256]{1,0:T(8,128)S(1)}, f32[320,256]{1,0:T(8,128)S(1)}, u32[]{:S(2)}, u32[]{:S(2)}) collective-permute-start(f32[320,256]{1,0:T(8,128)S(1)} %get-tuple-element.28.c0), channel_id=1, source_target_pairs={{0,64},{16,80},{32,96},{48,112},{64,0},{80,16},{96,32},{112,48},{1... | collective-permute-start | bytes 983048 | tf_op jit(solution)/shard_map/ppermute | solution.py:332
  68.0 17.8 %collective-permute-start.24 = (f32[320,256]{1,0:T(8,128)S(1)}, f32[320,256]{1,0:T(8,128)S(1)}, u32[]{:S(2)}, u32[]{:S(2)}) collective-permute-start(f32[320,256]{1,0:T(8,128)S(1)} %get-tuple-element.28.c0), channel_id=1, source_target_pairs={{0,128},{16,144},{32,160},{48,176},{64,192},{80,208},{96,224},{112... | collective-permute-start | bytes 983048 | tf_op jit(solution)/shard_map/ppermute | solution.py:332
  70.9 17.1 %collective-permute-start.25 = (f32[320,256]{1,0:T(8,128)S(1)}, f32[320,256]{1,0:T(8,128)S(1)}, u32[]{:S(2)}, u32[]{:S(2)}) collective-permute-start(f32[320,256]{1,0:T(8,128)S(1)} %get-tuple-element.28.c0), channel_id=1, source_target_pairs={{0,192},{16,208},{32,224},{48,240},{64,128},{80,144},{96,160},{112... | collective-permute-start | bytes 983048 | tf_op jit(solution)/shard_map/ppermute | solution.py:332
  98.2 18.9 %collective-permute-start.31 = (f32[4,2,112,256]{3,2,1,0:T(8,128)S(1)}, f32[4,2,112,256]{3,2,1,0:T(8,128)S(1)}, u32[]{:S(2)}, u32[]{:S(2)}) collective-permute-start(f32[4,2,112,256]{3,2,1,0:T(8,128)S(1)} %slice_bitcast_fusion), channel_id=1, source_target_pairs={{0,1},{1,0},{2,3},{3,2},{4,5},{5,4},{6,7},{7,6},{8,9},{9,8},{10,11... | collective-permute-start | bytes 2752520 | tf_op jit(solution)/shard_map/ppermute | solution.py:332
  99.9 10.0 %collective-permute-start.36 = (f32[4,64,256]{2,1,0:T(8,128)S(1)}, f32[4,64,256]{2,1,0:T(8,128)S(1)}, u32[]{:S(2)}, u32[]{:S(2)}) collective-permute-start(f32[4,64,256]{2,1,0:T(8,128)S(1)} %get-tuple-element.38), channel_id=1, source_target_pairs={{0,16},{16,0},{32,48},{48,32},{64,80},{80,64},{96,112},{112,96},{1... | collective-permute-start | bytes 786440 | tf_op jit(solution)/shard_map/ppermute | solution.py:332
  100.1 14.9 %collective-permute-start.37 = (f32[4,64,256]{2,1,0:T(8,128)S(1)}, f32[4,64,256]{2,1,0:T(8,128)S(1)}, u32[]{:S(2)}, u32[]{:S(2)}) collective-permute-start(f32[4,64,256]{2,1,0:T(8,128)S(1)} %get-tuple-element.40), channel_id=1, source_target_pairs={{0,32},{16,48},{32,0},{48,16},{64,96},{80,112},{96,64},{112,80},{1... | collective-permute-start | bytes 786440 | tf_op jit(solution)/shard_map/ppermute | solution.py:332
  102.9 14.1 %collective-permute-start.38 = (f32[4,64,256]{2,1,0:T(8,128)S(1)}, f32[4,64,256]{2,1,0:T(8,128)S(1)}, u32[]{:S(2)}, u32[]{:S(2)}) collective-permute-start(f32[4,64,256]{2,1,0:T(8,128)S(1)} %get-tuple-element.39), channel_id=1, source_target_pairs={{0,48},{16,32},{32,16},{48,0},{64,112},{80,96},{96,80},{112,64},{1... | collective-permute-start | bytes 786440 | tf_op jit(solution)/shard_map/ppermute | solution.py:332
  106.2 38.6 %collective-permute-start.44 = (f32[48,256]{1,0:T(8,128)S(1)}, f32[48,256]{1,0:T(8,128)S(1)}, u32[]{:S(2)}, u32[]{:S(2)}) collective-permute-start(f32[48,256]{1,0:T(8,128)S(1)} %get-tuple-element.44), channel_id=1, source_target_pairs={{0,2},{1,3},{16,18},{17,19},{32,34},{33,35},{48,50},{49,51},{64,66... | collective-permute-start | bytes 147464 | tf_op jit(solution)/shard_map/ppermute | solution.py:393
  109.9 36.2 %collective-permute-start.45 = (f32[48,256]{1,0:T(8,128)S(1)}, f32[48,256]{1,0:T(8,128)S(1)}, u32[]{:S(2)}, u32[]{:S(2)}) collective-permute-start(f32[48,256]{1,0:T(8,128)S(1)} %get-tuple-element.49), channel_id=1, source_target_pairs={{0,4},{1,5},{16,20},{17,21},{32,36},{33,37},{48,52},{49,53},{64,68... | collective-permute-start | bytes 147464 | tf_op jit(solution)/shard_map/ppermute | solution.py:393
  117.3 8.7 %collective-permute-start.32 = (f32[2,112,256]{2,1,0:T(8,128)S(1)}, f32[2,112,256]{2,1,0:T(8,128)S(1)}, u32[]{:S(2)}, u32[]{:S(2)}) collective-permute-start(f32[2,112,256]{2,1,0:T(8,128)S(1)} %get-tuple-element.41), channel_id=1, source_target_pairs={{0,2},{1,3},{2,0},{3,1},{4,6},{5,7},{6,4},{7,5},{8,10},{9,11},{10,... | collective-permute-start | bytes 688136 | tf_op jit(solution)/shard_map/ppermute | solution.py:332
  119.1 10.0 %collective-permute-start.33 = (f32[2,112,256]{2,1,0:T(8,128)S(1)}, f32[2,112,256]{2,1,0:T(8,128)S(1)}, u32[]{:S(2)}, u32[]{:S(2)}) collective-permute-start(f32[2,112,256]{2,1,0:T(8,128)S(1)} %get-tuple-element.43), channel_id=1, source_target_pairs={{0,4},{1,5},{2,6},{3,7},{4,0},{5,1},{6,2},{7,3},{8,12},{9,13},{10,... | collective-permute-start | bytes 688136 | tf_op jit(solution)/shard_map/ppermute | solution.py:332
  120.6 14.7 %collective-permute-start.34 = (f32[2,112,256]{2,1,0:T(8,128)S(1)}, f32[2,112,256]{2,1,0:T(8,128)S(1)}, u32[]{:S(2)}, u32[]{:S(2)}) collective-permute-start(f32[2,112,256]{2,1,0:T(8,128)S(1)} %get-tuple-element.42), channel_id=1, source_target_pairs={{0,6},{1,7},{2,4},{3,5},{4,2},{5,3},{6,0},{7,1},{8,14},{9,15},{10,... | collective-permute-start | bytes 688136 | tf_op jit(solution)/shard_map/ppermute | solution.py:332
  126.0 21.4 %collective-permute-start.46 = (f32[48,256]{1,0:T(8,128)S(1)}, f32[48,256]{1,0:T(8,128)S(1)}, u32[]{:S(2)}, u32[]{:S(2)}) collective-permute-start(f32[48,256]{1,0:T(8,128)S(1)} %get-tuple-element.48), channel_id=1, source_target_pairs={{0,6},{1,7},{16,22},{17,23},{32,38},{33,39},{48,54},{49,55},{64,70... | collective-permute-start | bytes 147464 | tf_op jit(solution)/shard_map/ppermute | solution.py:393
  129.0 19.7 %collective-permute-start.47 = (f32[48,256]{1,0:T(8,128)S(1)}, f32[48,256]{1,0:T(8,128)S(1)}, u32[]{:S(2)}, u32[]{:S(2)}) collective-permute-start(f32[48,256]{1,0:T(8,128)S(1)} %get-tuple-element.47), channel_id=1, source_target_pairs={{0,8},{1,9},{16,24},{17,25},{32,40},{33,41},{48,56},{49,57},{64,72... | collective-permute-start | bytes 147464 | tf_op jit(solution)/shard_map/ppermute | solution.py:393
  135.3 13.6 %collective-permute-start.48 = (f32[48,256]{1,0:T(8,128)S(1)}, f32[48,256]{1,0:T(8,128)S(1)}, u32[]{:S(2)}, u32[]{:S(2)}) collective-permute-start(f32[48,256]{1,0:T(8,128)S(1)} %get-tuple-element.46), channel_id=1, source_target_pairs={{0,10},{1,11},{16,26},{17,27},{32,42},{33,43},{48,58},{49,59},{64,... | collective-permute-start | bytes 147464 | tf_op jit(solution)/shard_map/ppermute | solution.py:393
  147.5 209.4 %collective-permute-start.72 = (f32[256,256]{1,0:T(8,128)}, f32[256,256]{1,0:T(8,128)}, u32[]{:S(2)}, u32[]{:S(2)}) collective-permute-start(f32[256,256]{1,0:T(8,128)} %slice_bitcast_fusion.2), channel_id=1, source_target_pairs={{16,0},{17,1},{18,2},{19,3},{20,4},{21,5},{22,6},{23,7},{24,8},{25... | collective-permute-start | bytes 786440 | tf_op jit(solution)/shard_map/ppermute | solution.py:397
  148.8 65.5 %collective-permute-start.26 = (f32[64,256]{1,0:T(8,128)S(1)}, f32[64,256]{1,0:T(8,128)S(1)}, u32[]{:S(2)}, u32[]{:S(2)}) collective-permute-start(f32[64,256]{1,0:T(8,128)S(1)} %slice_add_fusion.7), channel_id=1, source_target_pairs={{0,8},{1,9},{2,10},{3,11},{4,12},{5,13},{6,14},{7,15},{8,0},{9,1},... | collective-permute-start | bytes 196616 | tf_op jit(solution)/shard_map/ppermute | solution.py:332
  148.9 30.0 %collective-permute-start.39 = (f32[64,256]{1,0:T(8,128)S(1)}, f32[64,256]{1,0:T(8,128)S(1)}, u32[]{:S(2)}, u32[]{:S(2)}) collective-permute-start(f32[64,256]{1,0:T(8,128)S(1)} %get-tuple-element.64), channel_id=1, source_target_pairs={{0,64},{16,80},{32,96},{48,112},{64,0},{80,16},{96,32},{112,48},{1... | collective-permute-start | bytes 196616 | tf_op jit(solution)/shard_map/ppermute | solution.py:332
  149.0 31.3 %collective-permute-start.40 = (f32[64,256]{1,0:T(8,128)S(1)}, f32[64,256]{1,0:T(8,128)S(1)}, u32[]{:S(2)}, u32[]{:S(2)}) collective-permute-start(f32[64,256]{1,0:T(8,128)S(1)} %get-tuple-element.66), channel_id=1, source_target_pairs={{0,128},{16,144},{32,160},{48,176},{64,192},{80,208},{96,224},{112... | collective-permute-start | bytes 196616 | tf_op jit(solution)/shard_map/ppermute | solution.py:332
  150.3 26.3 %collective-permute-start.35 = (f32[112,256]{1,0:T(8,128)S(1)}, f32[112,256]{1,0:T(8,128)S(1)}, u32[]{:S(2)}, u32[]{:S(2)}) collective-permute-start(f32[112,256]{1,0:T(8,128)S(1)} %slice_bitcast_fusion.10), channel_id=1, source_target_pairs={{0,8},{1,9},{2,10},{3,11},{4,12},{5,13},{6,14},{7,15},{8,0},{9,1},... | collective-permute-start | bytes 344072 | tf_op jit(solution)/shard_map/ppermute | solution.py:332
  180.3 7.6 %collective-permute-start.52 = (f32[96,256]{1,0:T(8,128)S(1)}, f32[96,256]{1,0:T(8,128)S(1)}, u32[]{:S(2)}, u32[]{:S(2)}) collective-permute-start(f32[96,256]{1,0:T(8,128)S(1)} %pad_maximum_fusion.14), channel_id=1, source_target_pairs={{0,32},{16,48},{32,0},{48,16},{64,96},{80,112},{96,64},{112,80},{1... | collective-permute-start | bytes 294920 | tf_op jit(solution)/shard_map/ppermute | solution.py:332
  183.4 6.9 %collective-permute-start.42 = (f32[64,256]{1,0:T(8,128)S(1)}, f32[64,256]{1,0:T(8,128)S(1)}, u32[]{:S(2)}, u32[]{:S(2)}) collective-permute-start(f32[64,256]{1,0:T(8,128)S(1)} %fusion.16), channel_id=1, source_target_pairs={{0,0},{16,1},{1,16},{17,17},{2,32},{18,33},{3,48},{19,49},{4,64},{... | collective-permute-start | bytes 196616 | tf_op jit(solution)/shard_map/ppermute | solution.py:430
  188.5 9.8 %collective-permute-start.54 = (f32[96,256]{1,0:T(8,128)S(1)}, f32[96,256]{1,0:T(8,128)S(1)}, u32[]{:S(2)}, u32[]{:S(2)}) collective-permute-start(f32[96,256]{1,0:T(8,128)S(1)} %add_add_fusion.1), channel_id=1, source_target_pairs={{0,64},{16,80},{32,96},{48,112},{64,0},{80,16},{96,32},{112,48},{1... | collective-permute-start | bytes 294920 | tf_op jit(solution)/shard_map/ppermute | solution.py:332
  188.6 9.7 %collective-permute-start.55 = (f32[96,256]{1,0:T(8,128)S(1)}, f32[96,256]{1,0:T(8,128)S(1)}, u32[]{:S(2)}, u32[]{:S(2)}) collective-permute-start(f32[96,256]{1,0:T(8,128)S(1)} %add_add_fusion.1), channel_id=1, source_target_pairs={{0,128},{16,144},{32,160},{48,176},{64,192},{80,208},{96,224},{112... | collective-permute-start | bytes 294920 | tf_op jit(solution)/shard_map/ppermute | solution.py:332
  190.2 10.1 %collective-permute-start.56 = (f32[96,256]{1,0:T(8,128)S(1)}, f32[96,256]{1,0:T(8,128)S(1)}, u32[]{:S(2)}, u32[]{:S(2)}) collective-permute-start(f32[96,256]{1,0:T(8,128)S(1)} %add_add_fusion.1), channel_id=1, source_target_pairs={{0,192},{16,208},{32,224},{48,240},{64,128},{80,144},{96,160},{112... | collective-permute-start | bytes 294920 | tf_op jit(solution)/shard_map/ppermute | solution.py:332
  200.4 33.8 %collective-permute-start.57 = (f32[160,256]{1,0:T(8,128)S(1)}, f32[160,256]{1,0:T(8,128)S(1)}, u32[]{:S(2)}, u32[]{:S(2)}) collective-permute-start(f32[160,256]{1,0:T(8,128)S(1)} %pad_maximum_fusion.3), channel_id=1, source_target_pairs={{2,0},{3,1},{18,16},{19,17},{34,32},{35,33},{50,48},{51,49},{66,64... | collective-permute-start | bytes 491528 | tf_op jit(solution)/shard_map/ppermute | solution.py:427
  201.7 18.8 %collective-permute-start.58 = (f32[64,256]{1,0:T(8,128)S(1)}, f32[64,256]{1,0:T(8,128)S(1)}, u32[]{:S(2)}, u32[]{:S(2)}) collective-permute-start(f32[64,256]{1,0:T(8,128)S(1)} %fusion.16), channel_id=1, source_target_pairs={{32,0},{48,1},{33,16},{49,17},{34,32},{50,33},{35,48},{51,49},{36,... | collective-permute-start | bytes 196616 | tf_op jit(solution)/shard_map/ppermute | solution.py:430
  214.3 135.8 %collective-permute-start.27 = (f32[2,2,32,256]{3,2,1,0:T(8,128)S(1)}, f32[2,2,32,256]{3,2,1,0:T(8,128)S(1)}, u32[]{:S(2)}, u32[]{:S(2)}) collective-permute-start(f32[2,2,32,256]{3,2,1,0:T(8,128)S(1)} %bitcast.136), channel_id=1, source_target_pairs={{0,2},{1,3},{2,0},{3,1},{4,6},{5,7},{6,4},{7,5},{8,10},{9,11},{10,... | collective-permute-start | bytes 393224 | tf_op jit(solution)/shard_map/ppermute | solution.py:332
  215.9 134.2 %collective-permute-start.28 = (f32[2,2,32,256]{3,2,1,0:T(8,128)S(1)}, f32[2,2,32,256]{3,2,1,0:T(8,128)S(1)}, u32[]{:S(2)}, u32[]{:S(2)}) collective-permute-start(f32[2,2,32,256]{3,2,1,0:T(8,128)S(1)} %bitcast.137), channel_id=1, source_target_pairs={{0,4},{1,5},{2,6},{3,7},{4,0},{5,1},{6,2},{7,3},{8,12},{9,13},{10,... | collective-permute-start | bytes 393224 | tf_op jit(solution)/shard_map/ppermute | solution.py:332
  220.5 20.2 %collective-permute-start.60 = (f32[64,256]{1,0:T(8,128)S(1)}, f32[64,256]{1,0:T(8,128)S(1)}, u32[]{:S(2)}, u32[]{:S(2)}) collective-permute-start(f32[64,256]{1,0:T(8,128)S(1)} %fusion.16), channel_id=1, source_target_pairs={{64,0},{80,1},{65,16},{81,17},{66,32},{82,33},{67,48},{83,49},{68,... | collective-permute-start | bytes 196616 | tf_op jit(solution)/shard_map/ppermute | solution.py:430
  234.2 19.5 %collective-permute-start.59 = (f32[160,256]{1,0:T(8,128)S(1)}, f32[160,256]{1,0:T(8,128)S(1)}, u32[]{:S(2)}, u32[]{:S(2)}) collective-permute-start(f32[160,256]{1,0:T(8,128)S(1)} %pad_maximum_fusion.3), channel_id=1, source_target_pairs={{4,0},{5,1},{20,16},{21,17},{36,32},{37,33},{52,48},{53,49},{68,64... | collective-permute-start | bytes 491528 | tf_op jit(solution)/shard_map/ppermute | solution.py:427
  240.6 21.0 %collective-permute-start.62 = (f32[64,256]{1,0:T(8,128)S(1)}, f32[64,256]{1,0:T(8,128)S(1)}, u32[]{:S(2)}, u32[]{:S(2)}) collective-permute-start(f32[64,256]{1,0:T(8,128)S(1)} %fusion.16), channel_id=1, source_target_pairs={{96,0},{112,1},{97,16},{113,17},{98,32},{114,33},{99,48},{115,49},... | collective-permute-start | bytes 196616 | tf_op jit(solution)/shard_map/ppermute | solution.py:430
  253.6 19.2 %collective-permute-start.61 = (f32[160,256]{1,0:T(8,128)S(1)}, f32[160,256]{1,0:T(8,128)S(1)}, u32[]{:S(2)}, u32[]{:S(2)}) collective-permute-start(f32[160,256]{1,0:T(8,128)S(1)} %pad_maximum_fusion.3), channel_id=1, source_target_pairs={{6,0},{7,1},{22,16},{23,17},{38,32},{39,33},{54,48},{55,49},{70,64... | collective-permute-start | bytes 491528 | tf_op jit(solution)/shard_map/ppermute | solution.py:427
  261.7 19.2 %collective-permute-start.64 = (f32[64,256]{1,0:T(8,128)S(1)}, f32[64,256]{1,0:T(8,128)S(1)}, u32[]{:S(2)}, u32[]{:S(2)}) collective-permute-start(f32[64,256]{1,0:T(8,128)S(1)} %fusion.16), channel_id=1, source_target_pairs={{128,0},{144,1},{129,16},{145,17},{130,32},{146,33},{131,48},{147,... | collective-permute-start | bytes 196616 | tf_op jit(solution)/shard_map/ppermute | solution.py:430
  272.9 22.2 %collective-permute-start.63 = (f32[160,256]{1,0:T(8,128)S(1)}, f32[160,256]{1,0:T(8,128)S(1)}, u32[]{:S(2)}, u32[]{:S(2)}) collective-permute-start(f32[160,256]{1,0:T(8,128)S(1)} %pad_maximum_fusion.3), channel_id=1, source_target_pairs={{8,0},{9,1},{24,16},{25,17},{40,32},{41,33},{56,48},{57,49},{72,64... | collective-permute-start | bytes 491528 | tf_op jit(solution)/shard_map/ppermute | solution.py:427
  280.8 23.8 %collective-permute-start.66 = (f32[64,256]{1,0:T(8,128)S(1)}, f32[64,256]{1,0:T(8,128)S(1)}, u32[]{:S(2)}, u32[]{:S(2)}) collective-permute-start(f32[64,256]{1,0:T(8,128)S(1)} %fusion.16), channel_id=1, source_target_pairs={{160,0},{176,1},{161,16},{177,17},{162,32},{178,33},{163,48},{179,... | collective-permute-start | bytes 196616 | tf_op jit(solution)/shard_map/ppermute | solution.py:430
  295.1 22.0 %collective-permute-start.65 = (f32[160,256]{1,0:T(8,128)S(1)}, f32[160,256]{1,0:T(8,128)S(1)}, u32[]{:S(2)}, u32[]{:S(2)}) collective-permute-start(f32[160,256]{1,0:T(8,128)S(1)} %pad_maximum_fusion.3), channel_id=1, source_target_pairs={{10,0},{11,1},{26,16},{27,17},{42,32},{43,33},{58,48},{59,49},{74,... | collective-permute-start | bytes 491528 | tf_op jit(solution)/shard_map/ppermute | solution.py:427
  304.6 20.1 %collective-permute-start.68 = (f32[64,256]{1,0:T(8,128)S(1)}, f32[64,256]{1,0:T(8,128)S(1)}, u32[]{:S(2)}, u32[]{:S(2)}) collective-permute-start(f32[64,256]{1,0:T(8,128)S(1)} %fusion.16), channel_id=1, source_target_pairs={{192,0},{208,1},{193,16},{209,17},{194,32},{210,33},{195,48},{211,... | collective-permute-start | bytes 196616 | tf_op jit(solution)/shard_map/ppermute | solution.py:430
  317.0 21.9 %collective-permute-start.67 = (f32[160,256]{1,0:T(8,128)S(1)}, f32[160,256]{1,0:T(8,128)S(1)}, u32[]{:S(2)}, u32[]{:S(2)}) collective-permute-start(f32[160,256]{1,0:T(8,128)S(1)} %pad_maximum_fusion.3), channel_id=1, source_target_pairs={{12,0},{13,1},{28,16},{29,17},{44,32},{45,33},{60,48},{61,49},{76,... | collective-permute-start | bytes 491528 | tf_op jit(solution)/shard_map/ppermute | solution.py:427
  324.7 23.5 %collective-permute-start.70 = (f32[64,256]{1,0:T(8,128)S(1)}, f32[64,256]{1,0:T(8,128)S(1)}, u32[]{:S(2)}, u32[]{:S(2)}) collective-permute-start(f32[64,256]{1,0:T(8,128)S(1)} %fusion.16), channel_id=1, source_target_pairs={{224,0},{240,1},{225,16},{241,17},{226,32},{242,33},{227,48},{243,... | collective-permute-start | bytes 196616 | tf_op jit(solution)/shard_map/ppermute | solution.py:430
  339.0 9.3 %collective-permute-start.69 = (f32[160,256]{1,0:T(8,128)S(1)}, f32[160,256]{1,0:T(8,128)S(1)}, u32[]{:S(2)}, u32[]{:S(2)}) collective-permute-start(f32[160,256]{1,0:T(8,128)S(1)} %pad_maximum_fusion.3), channel_id=1, source_target_pairs={{14,0},{15,1},{30,16},{31,17},{46,32},{47,33},{62,48},{63,49},{78,... | collective-permute-start | bytes 491528 | tf_op jit(solution)/shard_map/ppermute | solution.py:427
  348.5 56.4 %collective-permute-start.71 = (f32[1280,256]{1,0:T(8,128)S(1)}, f32[1280,256]{1,0:T(8,128)}, u32[]{:S(2)}, u32[]{:S(2)}) collective-permute-start(f32[1280,256]{1,0:T(8,128)S(1)} %constant_dynamic-update-slice_fusion.10.mine), channel_id=1, source_target_pairs={{0,1},{1,0},{2,3},{3,2},{4,5},{5,4},{6,7},{7,6},{8,9},{9,8},{10,11... | collective-permute-start | bytes 3932168 | tf_op jit(solution)/shard_map/ppermute | solution.py:332
  355.3 12.6 %collective-permute-start.30 = (f32[2,256,256]{2,1,0:T(8,128)S(1)}, f32[2,256,256]{2,1,0:T(8,128)}, u32[]{:S(2)}, u32[]{:S(2)}) collective-permute-start(f32[2,256,256]{2,1,0:T(8,128)S(1)} %bitcast.135), channel_id=1, source_target_pairs={{0,1},{1,0},{2,3},{3,2},{4,5},{5,4},{6,7},{7,6},{8,9},{9,8},{10,11... | collective-permute-start | bytes 1572872 | tf_op jit(solution)/shard_map/ppermute | solution.py:332
  357.9 47.0 %collective-permute-start.73 = (f32[256,256]{1,0:T(8,128)S(1)}, f32[256,256]{1,0:T(8,128)S(1)}, u32[]{:S(2)}, u32[]{:S(2)}) collective-permute-start(f32[256,256]{1,0:T(8,128)S(1)} %broadcast_select_fusion.ea), channel_id=1, source_target_pairs={{0,1},{1,0},{2,3},{3,2},{4,5},{5,4},{6,7},{7,6},{8,9},{9,8},{10,11... | collective-permute-start | bytes 786440 | tf_op jit(solution)/shard_map/ppermute | solution.py:332
  (17 other events, 159.6 us)
